TPU v7x, 128 devices: a whole 4x4x4 slice. The times are simulated.
128 devices in a mesh: front: 8 (over x, core), row: 4 (over z), col: 4 (over y).
Axes of the slice: x: 4, y: 4, z: 4, core: 2. Of those that a mesh axis runs over, the one named last changes fastest.
Arguments:
- parent_front: float32 [8, 4096, 4096], P('front', 'row', 'col'), may hold values from -6 to 6
- child_tiles: float32 [4096, 256, 256], P(('front', 'row', 'col')), may hold values from -6 to 6
- destination: int32 [4096, 1], P(('front', 'row', 'col')), may hold values from 0 to 31; in each aligned block of 32 rows (0 to 31, 32 to 63, ...) at most 2 rows name the same one
- row_map: int32 [4096, 256], P(('front', 'row', 'col')), may hold values from 0 to 1023, as said below
- col_map: int32 [4096, 256], P(('front', 'row', 'col')), may hold values from 0 to 1023, as said below
- pivot_inverse: float32 [8, 2, 256, 256], P('front')
Outputs:
- factored: float32 [8, 4096, 4096], P('front', 'row', 'col')
Inputs may be any that keep to these rules, and one draw needn't show every extreme that they name: `destination`: in each device's block of 32 rows no value appears more than 2 times. `row_map`: each row's entries are distinct and lie in one aligned block of 256. `col_map`: each row's entries are distinct and lie in one aligned block of 256.
All inputs are finite; a program needn't handle non-finite values.
Results may differ from a plain program's by a relative error of at most 0.00014.
Values sent between devices are 32-bit elements; how exact they have to be, the bound alone decides.
No kernel may reach another device: no remote copies, remote signals or barrier semaphores. Data moves between devices by JAX's collectives and lax.ppermute only.
A program may use at most 128 MiB of HBM per device.

v0:
```python
import jax
import jax.numpy as jnp
from jax import lax
from jax.sharding import PartitionSpec as P

PANELS = 2


def spread(value, axis, source):
    kept = jnp.where(lax.axis_index(axis) == source, value, 0).astype(value.dtype)
    return lax.psum(kept, axis)


def permute_tiles(values, rows_in, cols_in):
    width = values.shape[-1]
    positions = jnp.arange(width, dtype=jnp.int32)
    row_onehot = (rows_in[..., None] % width == positions).astype(jnp.float32)
    col_onehot = (cols_in[..., None] % width == positions).astype(jnp.float32)
    moved = jnp.einsum(
        "...ia,...ij->...aj",
        row_onehot,
        values,
        precision=lax.Precision.HIGHEST,
        preferred_element_type=jnp.float32,
    )
    return jnp.einsum(
        "...aj,...jb->...ab",
        moved,
        col_onehot,
        precision=lax.Precision.HIGHEST,
        preferred_element_type=jnp.float32,
    )


def per_device(parent_front, child_tiles, destination, row_map, col_map, pivot_inverse):
    count = child_tiles.shape[0]
    width = child_tiles.shape[1]
    matrix = parent_front[0]
    rows_blk = matrix.shape[0]
    cols_blk = matrix.shape[1]
    tiles_down = rows_blk // width
    tiles_across = cols_blk // width
    fronts_n = lax.axis_size("front")
    rows_n = lax.axis_size("row")
    targets = fronts_n * rows_n
    capacity = 2 * count // targets
    target = destination[:, 0]
    order = jnp.arange(count, dtype=jnp.int32)
    same = target[:, None] == target[None, :]
    earlier = order[None, :] < order[:, None]
    slot = jnp.sum((same & earlier).astype(jnp.int32), axis=1)
    both_maps = jnp.stack([row_map, col_map], axis=1)
    send_tiles = (
        jnp.zeros((targets, capacity, width, width), jnp.float32).at[target, slot].set(child_tiles)
    )
    send_maps = jnp.zeros((targets, capacity, 2, width), jnp.int32).at[target, slot].set(both_maps)
    values = lax.all_to_all(send_tiles, ("front", "row"), split_axis=0, concat_axis=0, tiled=True)
    maps_in = lax.all_to_all(send_maps, ("front", "row"), split_axis=0, concat_axis=0, tiled=True)
    values = permute_tiles(values, maps_in[:, :, 0, :], maps_in[:, :, 1, :])
    where_to = maps_in[:, :, 0, 0] // width * tiles_across + maps_in[:, :, 1, 0] // width
    onehot = (where_to[..., None] == jnp.arange(tiles_down * tiles_across, dtype=jnp.int32)).astype(
        jnp.float32
    )
    placed = jnp.einsum(
        "sni,snab->niab",
        onehot,
        values,
        precision=lax.Precision.HIGHEST,
        preferred_element_type=jnp.float32,
    )
    summed = jnp.sum(placed, axis=0).reshape(tiles_down, tiles_across, width, width)
    summed = summed.transpose(0, 2, 1, 3).reshape(rows_blk, cols_blk)
    matrix = matrix + summed
    row_index = lax.axis_index("row")
    col_index = lax.axis_index("col")
    global_rows = row_index * rows_blk + jnp.arange(rows_blk, dtype=jnp.int32)
    global_cols = col_index * cols_blk + jnp.arange(cols_blk, dtype=jnp.int32)
    for panel in range(PANELS):
        start = panel * width
        stop = start + width
        root_col = start // cols_blk
        local_col = start % cols_blk
        root_row = start // rows_blk
        local_row = start % rows_blk
        inverse_now = pivot_inverse[0, panel]
        columns = matrix[:, local_col : local_col + width]
        arrived = spread(columns, "col", root_col)
        factor = jnp.dot(
            arrived,
            inverse_now,
            precision=lax.Precision.HIGHEST,
            preferred_element_type=jnp.float32,
        )
        pivot_rows = spread(matrix[local_row : local_row + width, :], "row", root_row)
        update = jnp.dot(
            factor, pivot_rows, precision=lax.Precision.HIGHEST, preferred_element_type=jnp.float32
        )
        trailing = (global_rows >= stop)[:, None] & (global_cols >= stop)[None, :]
        matrix = jnp.where(trailing, matrix - update, matrix)
        keep_factor = ((col_index == root_col) & (global_rows >= stop))[:, None]
        current = matrix[:, local_col : local_col + width]
        matrix = matrix.at[:, local_col : local_col + width].set(
            jnp.where(keep_factor, factor, current)
        )
    return matrix[None]


def solution(mesh):
    in_specs = (
        P("front", "row", "col"),
        P(("front", "row", "col"), None, None),
        P(("front", "row", "col"), None),
        P(("front", "row", "col"), None),
        P(("front", "row", "col"), None),
        P("front", None, None, None),
    )
    out_specs = P("front", "row", "col")
    return jax.shard_map(
        per_device, mesh=mesh, in_specs=in_specs, out_specs=out_specs, check_vma=False
    )
```

profile of v0, /device:TPU:0, one launch (start us, length us, event | category | flops | bytes accessed | tf_op | source)
XLA Modules:
  0.0 570.0 jit_solution(8545701261372075921)
XLA Ops:
  6.5 0.9 convert_reduce_fusion
  7.4 0.7 fusion.30
  8.1 0.8 pad_add_fusion
  8.9 0.1 copy.15
  8.9 0.7 broadcast_in_dim.50
  9.6 3.8 scatter_fusion
  13.4 8.2 %all-to-all-start = ((s32[32,2,2,256]{3,2,1,0:T(2,128)}), s32[32,2,2,256]{3,2,1,0:T(2,128)S(1)}, u32[]{:S(2)}, u32[]{:S(2)}) async-start(s32[32,2,2,256]{3,2,1,0:T(2,128)} %scatter_fusion), calls=%async_computation | async-start | bytes 262144 | tf_op jit(solution)/shard_map/all_to_all | solution.py:58
  21.7 7.8 %broadcast_in_dim.51 = f32[32,2,256,256]{3,2,1,0:T(8,128)} broadcast(f32[]{:T(128)} %constant.117.clone.1), dimensions={} | broadcast | bytes 16777220 | tf_op jit(solution)/shard_map/broadcast_in_dim | solution.py:54
  29.4 15.4 %scatter_fusion.1 = f32[32,2,256,256]{3,2,1,0:T(8,128)} fusion(f32[32,2,256,256]{3,2,1,0:T(8,128)} %broadcast_in_dim.51, s32[32]{0:T(128)S(1)} %fusion.30, f32[32,256,256]{2,1,0:T(8,128)} %param.11), kind=kCustom, calls=%fused_computation.1 | custom fusion | bytes 25166080 | tf_op jit(solution)/shard_map/scatter | solution.py:54
  44.9 7.5 %all-to-all-start.1 = ((f32[32,2,256,256]{3,2,1,0:T(8,128)}), f32[32,2,256,256]{3,2,1,0:T(8,128)}, u32[]{:S(2)}, u32[]{:S(2)}) async-start(f32[32,2,256,256]{3,2,1,0:T(8,128)} %scatter_fusion.1), calls=%async_computation.1 | async-start | bytes 33554432 | tf_op jit(solution)/shard_map/all_to_all | solution.py:57
  52.4 0.2 all-reduce.5.cloned.1.call-start
  52.6 0.1 fusion.31
  52.7 0.1 copy.16
  52.8 0.1 copy.17
  52.9 0.1 fusion.32
  53.0 0.2 and_select_fusion
  53.2 221.2 %all-to-all-done.1 = f32[32,2,256,256]{3,2,1,0:T(8,128)} async-done(((f32[32,2,256,256]{3,2,1,0:T(8,128)}), f32[32,2,256,256]{3,2,1,0:T(8,128)}, u32[]{:S(2)}, u32[]{:S(2)}) %all-to-all-start.1) | async-done | bytes 16777248 | tf_op jit(solution)/shard_map/all_to_all | solution.py:57
  274.4 22.4 %fusion.2 = f32[32,2,256,256]{3,2,1,0:T(8,128)} fusion(f32[32,2,256,256]{3,2,1,0:T(8,128)} %all-to-all-done.1, s32[32,2,256]{2,1,0:T(2,128)S(1)} %get-tuple-element.34), kind=kOutput, calls=%fused_computation.6 | convolution fusion | flops 12889096192 | bytes 33619968 | tf_op jit(solution)/shard_map/...ia,...ij->...aj/dot_general | solution.py:19
  296.9 13.6 %fusion.3 = f32[32,2,256,256]{3,2,1,0:T(8,128)S(1)} fusion(f32[32,2,256,256]{3,2,1,0:T(8,128)} %fusion.2, s32[32,2,256]{2,1,0:T(2,128)S(1)} %get-tuple-element.33), kind=kOutput, calls=%fused_computation.7 | convolution fusion | flops 12889096192 | bytes 33619968 | tf_op jit(solution)/shard_map/...aj,...jb->...ab/dot_general | solution.py:26
  310.5 13.0 %fusion.6 = f32[16,256,256]{2,0,1:T(8,128)} fusion(f32[32,2,256,256]{3,2,1,0:T(8,128)S(1)} %fusion.3, s32[32,2]{0,1:T(2,128)S(1)} %fusion.28), kind=kOutput, calls=%fused_computation.13 | convolution fusion | flops 805307392 | bytes 20971776 | tf_op jit(solution)/shard_map/sni,snab->niab/dot_general | solution.py:64
  323.4 5.2 reshape.207
  328.6 2.9 copy.20
  331.5 1.0 copy.24
  332.6 1.1 copy-done.2
  333.7 1.4 bitcast_add_fusion
  335.1 2.0 copy-done.1
  337.1 1.1 slice_select_fusion.3
  338.2 0.0 all-reduce.5.cloned.1.call-update
  338.3 0.0 all-reduce.7.cloned.1.call-start
  338.3 2.3 slice_select_fusion.2
  340.7 0.0 all-reduce.9.cloned.1.call-start
  340.7 0.7 compare_reduce_fusion.1
  341.4 56.7 %all-reduce.5.cloned.1.call-done = f32[1024,256]{1,0:T(8,128)} async-done(((f32[1024,256]{1,0:T(8,128)}), f32[1024,256]{1,0:T(8,128)}) %all-reduce.5.cloned.1.call-update) | async-done | bytes 1048592 | tf_op jit(solution)/shard_map/psum | solution.py:11
  398.2 2.2 fusion.14
  400.4 47.3 %all-reduce.7.cloned.1.call-done = f32[256,1024]{1,0:T(8,128)} async-done(((f32[256,1024]{1,0:T(8,128)}), f32[256,1024]{1,0:T(8,128)}) %all-reduce.7.cloned.1.call-update) | async-done | bytes 1048592 | tf_op jit(solution)/shard_map/psum | solution.py:11
  447.6 6.1 %subtract_select_fusion.1 = f32[1024,1024]{1,0:T(8,128)S(1)} fusion(f32[1024,1024]{1,0:T(8,128)} %copy-done.1, f32[1024,256]{1,0:T(8,128)S(1)} %fusion.14, f32[256,1024]{1,0:T(8,128)} %all-reduce.7.cloned.1.call-done, pred[1024]{0:T(1024)(128)(4,1)S(1)} %get-tuple-element.35, pred[1024]{0:T(1024)(128)(4,1)S(1)} %get-tuple-element.36), kind=kOutput, calls=%fused_computation.11 | convolution fusion | flops 3224371200 | bytes 10487808 | tf_op jit(solution)/shard_map/dot_general | solution.py:95
  453.7 0.9 fusion.9
  454.6 2.0 copy-done
  456.6 1.1 slice_select_fusion.1
  457.7 0.0 all-reduce.11.cloned.1.call-start
  457.8 2.3 slice_select_fusion
  460.1 0.7 compare_reduce_fusion
  460.8 43.5 %all-reduce.9.cloned.1.call-done = f32[1024,256]{1,0:T(8,128)} async-done(((f32[1024,256]{1,0:T(8,128)}), f32[1024,256]{1,0:T(8,128)}) %all-reduce.9.cloned.1.call-update) | async-done | bytes 1048592 | tf_op jit(solution)/shard_map/psum | solution.py:11
  504.3 2.2 fusion.12
  506.5 47.1 %all-reduce.11.cloned.1.call-done = f32[256,1024]{1,0:T(8,128)} async-done(((f32[256,1024]{1,0:T(8,128)}), f32[256,1024]{1,0:T(8,128)}) %all-reduce.11.cloned.1.call-update) | async-done | bytes 1048592 | tf_op jit(solution)/shard_map/psum | solution.py:11
  553.6 6.0 %subtract_select_fusion = f32[1024,1024]{1,0:T(8,128)S(1)} fusion(f32[1024,1024]{1,0:T(8,128)} %copy-done, f32[1024,256]{1,0:T(8,128)S(1)} %fusion.12, f32[256,1024]{1,0:T(8,128)} %all-reduce.11.cloned.1.call-done, pred[1024]{0:T(1024)(128)(4,1)S(1)} %get-tuple-element.37, pred[1024]{0:T(1024)(128)(4,1)S(1)} %get-tuple-element.38), kind=kOutput, calls=%fused_computation.10 | convolution fusion | flops 3224371200 | bytes 10487808 | tf_op jit(solution)/shard_map/dot_general | solution.py:95
  559.7 2.0 copy.40
  561.7 1.8 fusion.11
  (14 shorter events, 0.1 us)
Async XLA Ops:
  13.4 31.5 %all-to-all-start = ((s32[32,2,2,256]{3,2,1,0:T(2,128)}), s32[32,2,2,256]{3,2,1,0:T(2,128)S(1)}, u32[]{:S(2)}, u32[]{:S(2)}) async-start(s32[32,2,2,256]{3,2,1,0:T(2,128)} %scatter_fusion), calls=%async_computation | async-start | bytes 262144 | tf_op jit(solution)/shard_map/all_to_all | solution.py:58
  44.9 229.6 %all-to-all-start.1 = ((f32[32,2,256,256]{3,2,1,0:T(8,128)}), f32[32,2,256,256]{3,2,1,0:T(8,128)}, u32[]{:S(2)}, u32[]{:S(2)}) async-start(f32[32,2,256,256]{3,2,1,0:T(8,128)} %scatter_fusion.1), calls=%async_computation.1 | async-start | bytes 33554432 | tf_op jit(solution)/shard_map/all_to_all | solution.py:57
  52.4 345.8 %all-reduce.5.cloned.1.call-start = ((), (), s32[]{:S(2)}) async-start(), calls=%async_computation.2 | async-start | bytes 2097152 | tf_op jit(solution)/shard_map/psum | solution.py:11
  331.5 2.2 copy-start.2
  335.1 2.0 copy-start.1
  337.1 61.1 %copy-start.3 = (f32[1,2,256,256]{3,2,1,0:T(8,128)S(1)}, f32[1,2,256,256]{3,2,1,0:T(8,128)}, u32[]{:S(2)}) copy-start(f32[1,2,256,256]{3,2,1,0:T(8,128)} %param.15) | copy-start | bytes 1572868
  338.3 109.4 %all-reduce.7.cloned.1.call-start = ((), (), s32[]{:S(2)}) async-start(), calls=%async_computation.3 | async-start | bytes 2097152 | tf_op jit(solution)/shard_map/psum | solution.py:11
  340.7 163.6 %all-reduce.9.cloned.1.call-start = ((), (), s32[]{:S(2)}) async-start(), calls=%async_computation.4 | async-start | bytes 2097152 | tf_op jit(solution)/shard_map/psum | solution.py:11
  454.6 2.0 copy-start
  457.7 95.9 %all-reduce.11.cloned.1.call-start = ((), (), s32[]{:S(2)}) async-start(), calls=%async_computation.5 | async-start | bytes 2097152 | tf_op jit(solution)/shard_map/psum | solution.py:11
Sparse Core Ops, SparseCore 0:
  338.4 59.7 all-reduce.4
  400.6 46.9 all-reduce.6
  457.9 46.3 all-reduce.8
  506.6 46.9 all-reduce.10
where the time goes:
time: 571 us; the launch traced here: 570 us
  waiting for transfers between devices  416 us (73%)
  matrix products  65.5 us (11%)
  local copies, waits for them, and re-layouts  44.4 us (8%)
  starting transfers between devices  16.1 us (3%)
  other arithmetic  14.8 us (3%)
  between operations  13.3 us (2%)
    all_to_all x1, waiting for transfers between devices, per_device(): lax.all_to_all(send_tiles, ('front', 'row'), split_axis=0, concat_axis=0,...  221 us
    psum x4, waiting for transfers between devices, spread(): return lax.psum(kept, axis)  195 us
    dot_general x1, matrix products, permute_tiles(): jnp.einsum('...ia,...ij->...aj', row_onehot, values, precision=lax.Precis...  22.4 us
    scatter x1, local copies, waits for them, and re-layouts, per_device(): jnp.zeros((targets, capacity, width, width), jnp.float32).at[target, slot]  15.4 us
    dot_general x1, matrix products, permute_tiles(): jnp.einsum('...aj,...jb->...ab', moved, col_onehot, precision=lax.Precisi...  13.6 us
    dot_general x1, matrix products, per_device(): jnp.einsum('sni,snab->niab', onehot, values, precision=lax.Precision.HIGH...  13 us
    dot_general x2, matrix products, per_device(): jnp.dot(factor, pivot_rows, precision=lax.Precision.HIGHEST, preferred_el...  12.1 us
  transfers between devices with their start and end apart: 6, of which 5 were waited for; matrix products, arithmetic and copies ran while one was open for 6% of the time, Pallas kernels for 0%

commit v1 on v0

v1 whole, which is shorter than its diff:
```python
import jax
import jax.numpy as jnp
from jax import lax
from jax.experimental import pallas as pl
from jax.experimental.pallas import tpu as pltpu
from jax.sharding import PartitionSpec as P

PLANE = ("front", "row")
W = 256
SUBS = 4
FULL = SUBS * W
HALF = 2 * W
STRIP = 8
NJ = 32
RING = 4
ANY = pl.BlockSpec(memory_space=pl.ANY)
VMEM = pl.BlockSpec(memory_space=pltpu.VMEM)
SMEM = pl.BlockSpec(memory_space=pltpu.SMEM)
DMA = pltpu.SemaphoreType.DMA


def f32(*shape):
    return jax.ShapeDtypeStruct(shape, jnp.float32)


def space(*shape, dtype=jnp.float32):
    return pltpu.VMEM(shape, dtype)


def params(flops, moved):
    return {
        "compiler_params": pltpu.CompilerParams(vmem_limit_bytes=62 * 1024 * 1024),
        "cost_estimate": pl.CostEstimate(flops=flops, bytes_accessed=moved, transcendentals=0),
    }


def split(value):
    high = value.astype(jnp.bfloat16)
    low = (value - high.astype(jnp.float32)).astype(jnp.bfloat16)
    return high, low


def dot(a, b):
    return jnp.dot(a, b, preferred_element_type=jnp.float32)


def dot3(a, b):
    ah, al = a
    bh, bl = b
    return dot(ah, bh) + (dot(ah, bl) + dot(al, bh))


def place_of(row, col):
    least = jnp.minimum(row, col)
    first = jnp.where(col == 0, row, 3 + col)
    second = jnp.where(col == 1, 6 + row, 8 + col)
    rest = 12 + (row - 2) * 2 + (col - 2)
    return jnp.where(least == 0, first, jnp.where(least == 1, second, rest))


PLACE = {}
for _r in range(SUBS):
    for _c in range(SUBS):
        PLACE[_r, _c] = (
            (_r if _c == 0 else 3 + _c)
            if min(_r, _c) == 0
            else (6 + _r if _c == 1 else 8 + _c)
            if min(_r, _c) == 1
            else 12 + (_r - 2) * 2 + _c - 2
        )


def permute_kernel(dest_ref, rows_ref, cols_ref, tiles_hbm, out_hbm, tiles, out, in_sems, out_sems):
    count = tiles.shape[0]
    groups = in_sems.shape[0]
    step = count // groups
    index = lax.broadcasted_iota(jnp.int32, (W, W), 0)
    contract = (((1,), (1,)), ((), ()))

    def load(g):
        at = pl.ds(g * step, step)
        return pltpu.make_async_copy(tiles_hbm.at[at], tiles.at[at], in_sems.at[g])

    def store(k, first, last):
        at = pl.ds(first, last - first)
        return pltpu.make_async_copy(out.at[:, at], out_hbm.at[:, at], out_sems.at[k])

    def work(g, carry):
        load(g).wait()
        for k in range(step):
            i = g * step + k
            rows = rows_ref[pl.ds(i, 1), :] & (W - 1)
            cols = cols_ref[pl.ds(i, 1), :] & (W - 1)
            row_hot = (index == rows).astype(jnp.float32).astype(jnp.bfloat16)
            col_hot = (index == cols).astype(jnp.float32).astype(jnp.bfloat16)
            high, low = split(tiles[i])
            high = lax.dot_general(high, col_hot, contract, preferred_element_type=jnp.float32)
            low = lax.dot_general(low, col_hot, contract, preferred_element_type=jnp.float32)
            moved = dot(row_hot, high.astype(jnp.bfloat16)) + dot(
                row_hot, low.astype(jnp.bfloat16)
            )
            out[:, i] = moved.reshape(NJ, STRIP, W)
        return carry

    for g in range(groups):
        load(g).start()
    place = place_of(rows_ref[:, :1] // W, cols_ref[:, :1] // W)
    place = place.astype(jnp.float32)
    same = lax.broadcasted_iota(jnp.int32, (count, W), 0) == lax.broadcasted_iota(
        jnp.int32, (count, W), 1
    )
    line = jnp.sum(jnp.where(same, place, 0.0), axis=0, keepdims=True)
    out[:, count] = jnp.broadcast_to(line[None], (NJ, STRIP, W))
    line = line[:, :count] + (dest_ref[...] * (SUBS * SUBS)).astype(jnp.float32)
    out[:, count, :, :count] = jnp.broadcast_to(line[None], (NJ, STRIP, count))
    half = groups // 2
    lax.fori_loop(0, half, work, 0)
    store(0, 0, half * step).start()
    lax.fori_loop(half, groups, work, 0)
    store(1, half * step, count + 1).start()
    store(0, 0, half * step).wait()
    store(1, half * step, count + 1).wait()


def permute_tiles(child_tiles, destination, row_map, col_map):
    count = child_tiles.shape[0]
    groups = 4
    return pl.pallas_call(
        permute_kernel,
        in_specs=[VMEM, VMEM, VMEM, ANY],
        out_specs=ANY,
        out_shape=f32(NJ, count + 1, STRIP, W),
        scratch_shapes=[
            space(count, W, W),
            space(NJ, count + 1, STRIP, W),
            DMA((groups,)),
            DMA((2,)),
        ],
        name="permute",
        **params(8 * count * W**3, 8 * count * W * W),
    )(destination.reshape(1, count), row_map, col_map, child_tiles)


def reduce_kernel(strips_hbm, out_hbm, strips, sums, lines, codes_vmem, codes, sems, sem):
    count = strips.shape[1]
    groups = sems.shape[0]
    step = NJ // groups

    def load(g):
        at = pl.ds(g * step, step)
        return pltpu.make_async_copy(
            strips_hbm.at[at, pl.ds(0, count)], strips.at[at], sems.at[g]
        )

    line_copy = pltpu.make_async_copy(
        strips_hbm.at[:, count, :, pl.ds(0, 128)], lines, sem.at[0]
    )
    line_copy.start()
    for g in range(groups):
        load(g).start()
    sums[...] = jnp.zeros_like(sums)
    line_copy.wait()
    codes_vmem[...] = lines[:, 0].astype(jnp.int32)
    code_copy = pltpu.make_async_copy(codes_vmem, codes, sem.at[1])
    code_copy.start()
    code_copy.wait()
    for g in range(groups):
        load(g).wait()

        def add(i, carry):
            source = g * step + i // (count // 8)
            tile = i % (count // 8) * 8
            for k in range(8):
                code = codes[source, tile + k]
                sums[code] = sums[code] + strips[source, tile + k]
            return carry

        lax.fori_loop(0, step * (count // 8), add, 0, unroll=2)
    done = pltpu.make_async_copy(sums, out_hbm, sem.at[2])
    done.start()
    done.wait()


def reduce_strips(strips, slots):
    count = strips.shape[1] - 1
    groups = 8
    return pl.pallas_call(
        reduce_kernel,
        in_specs=[ANY],
        out_specs=ANY,
        out_shape=f32(slots, STRIP, W),
        scratch_shapes=[
            space(NJ, count, STRIP, W),
            space(slots, STRIP, W),
            space(NJ, STRIP, 128),
            space(NJ, 128, dtype=jnp.int32),
            pltpu.SMEM((NJ, 128), jnp.int32),
            DMA((groups,)),
            DMA((3,)),
        ],
        name="reduce",
        **params(NJ * count * STRIP * W, 4 * (NJ * count + slots) * STRIP * W),
    )(strips)


def first_kernel(parent_hbm, got_hbm, inv_ref, *refs):
    outs, (column, pivot, got, left, right, sems, out_sems) = refs[:4], refs[4:]
    copies = [
        pltpu.make_async_copy(got_hbm.at[:, pl.ds(0, 7)], got, sems.at[0]),
        pltpu.make_async_copy(parent_hbm.at[:, pl.ds(0, W)], column, sems.at[1]),
        pltpu.make_async_copy(parent_hbm.at[pl.ds(0, W)], pivot, sems.at[2]),
    ]
    for copy in copies:
        copy.start()
    inv = split(inv_ref[0])
    for copy in copies:
        copy.wait()
    stores = halves(outs, left, right, out_sems)
    for k in range(SUBS):
        at = slice(k * W, (k + 1) * W)
        values = column[at] + got[:, PLACE[k, 0]].reshape(W, W)
        left[at] = dot3(split(values), inv)
        right[:, at] = pivot[:, at] + got[:, PLACE[0, k]].reshape(W, W)
        if k % 2:
            stores[k // 2].start()
            stores[2 + k // 2].start()
    for store in stores:
        store.wait()


def halves(outs, left, right, sems):
    parts = [
        left.at[pl.ds(0, HALF)],
        left.at[pl.ds(HALF, HALF)],
        right.at[:, pl.ds(0, HALF)],
        right.at[:, pl.ds(HALF, HALF)],
    ]
    return [pltpu.make_async_copy(parts[k], outs[k], sems.at[k]) for k in range(4)]


HALVES = [f32(HALF, W), f32(HALF, W), f32(W, HALF), f32(W, HALF)]


def first_panel(parent, got, inverses):
    return pl.pallas_call(
        first_kernel,
        in_specs=[ANY, ANY, VMEM],
        out_specs=[ANY] * 4,
        out_shape=HALVES,
        scratch_shapes=[
            space(FULL, W),
            space(W, FULL),
            space(NJ, 7, STRIP, W),
            space(FULL, W),
            space(W, FULL),
            DMA((3,)),
            DMA((4,)),
        ],
        name="first_panel",
        **params(6 * FULL * W * W, 24 * FULL * W),
    )(parent, got, inverses)


def assemble_kernel(parent_ref, got_ref, all_ref):
    step = pl.program_id(0)
    for r in range(SUBS):

        @pl.when(step == r)
        def _():
            for c in range(SUBS):
                at = slice(c * W, (c + 1) * W)
                all_ref[:, at] = parent_ref[:, at] + got_ref[:, PLACE[r, c]].reshape(W, W)


def assemble(parent, got):
    return pl.pallas_call(
        assemble_kernel,
        grid=(SUBS,),
        in_specs=[pl.BlockSpec((W, FULL), lambda i: (i, 0)), VMEM],
        out_specs=pl.BlockSpec((W, FULL), lambda i: (i, 0)),
        out_shape=f32(FULL, FULL),
        name="assemble",
        **params(FULL * FULL, 12 * FULL * FULL),
    )(parent, got)


def fetch(index, near, parts, target, sem):
    own, first, second = parts

    @pl.when(index == 0)
    def _():
        pltpu.make_async_copy(own, target, sem).start()

    @pl.when(index == near)
    def _():
        pltpu.make_async_copy(first, target, sem).start()

    @pl.when((index != 0) & (index != near))
    def _():
        pltpu.make_async_copy(second, target, sem).start()

    return pltpu.make_async_copy(own, target, sem)


def fetch_all(place_ref, pieces, left, right, sems):
    row, col = place_ref[0], place_ref[1]
    return [
        fetch(col, 1, pieces[0:3], left.at[pl.ds(0, HALF)], sems.at[0]),
        fetch(col, 3, pieces[3:6], left.at[pl.ds(HALF, HALF)], sems.at[1]),
        fetch(row, 1, pieces[6:9], right.at[:, pl.ds(0, HALF)], sems.at[2]),
        fetch(row, 3, pieces[9:12], right.at[:, pl.ds(HALF, HALF)], sems.at[3]),
    ]


def second_kernel(place_ref, *refs):
    pieces = refs[:12]
    matrix, inv_ref, *outs = refs[12:18]
    left, right, column, pivot, sems, out_sems = refs[18:]
    row, col = place_ref[0], place_ref[1]
    copies = fetch_all(place_ref, pieces, left, right, sems)
    copies.append(pltpu.make_async_copy(matrix.at[:, pl.ds(W, W)], column, sems.at[4]))
    copies.append(pltpu.make_async_copy(matrix.at[pl.ds(W, W)], pivot, sems.at[5]))
    for copy in copies[4:]:
        copy.start()
    for copy in copies:
        copy.wait()
    stores = halves(outs, column, pivot, out_sems)

    @pl.when(col == 0)
    def _():
        inv = split(inv_ref[1])
        corner = split(right[:, W:HALF])
        for k in range(SUBS):
            at = slice(k * W, (k + 1) * W)
            reduced = column[at] - dot3(split(left[at]), corner)
            column[at] = dot3(split(reduced), inv)
            if k % 2:
                stores[k // 2].start()

    @pl.when(row == 0)
    def _():
        below = split(left[W:HALF])
        for k in range(SUBS):
            at = slice(k * W, (k + 1) * W)
            pivot[:, at] = pivot[:, at] - dot3(below, split(right[:, at]))
            if k % 2:
                stores[2 + k // 2].start()

    @pl.when(col == 0)
    def _():
        stores[0].wait()
        stores[1].wait()

    @pl.when(row == 0)
    def _():
        stores[2].wait()
        stores[3].wait()


def second_panel(place, pieces, matrix, inverses):
    return pl.pallas_call(
        second_kernel,
        in_specs=[SMEM] + [ANY] * 13 + [VMEM],
        out_specs=[ANY] * 4,
        out_shape=HALVES,
        scratch_shapes=[
            space(FULL, W),
            space(W, FULL),
            space(FULL, W),
            space(W, FULL),
            DMA((6,)),
            DMA((4,)),
        ],
        name="second_panel",
        **params(18 * FULL * W * W, 32 * FULL * W),
    )(place, *pieces, matrix, inverses)


def update_kernel(panel, place_ref, *refs):
    pieces = refs[:12]
    matrix, out_hbm, left, right, high, low, held, sems, in_sems, out_sems = refs[12:]
    row, col = place_ref[0], place_ref[1]

    def copy(k, source, target, sem):
        at = pl.ds(k * W, W)
        return pltpu.make_async_copy(source.at[at], target.at[at], sem.at[k])

    copies = fetch_all(place_ref, pieces, left, right, sems)
    for k in range(SUBS):
        copy(k, matrix, held, in_sems).start()
    for c in (2, 3, 0, 1):
        copies[c].wait()
    values = split(right[...])
    high[...] = values[0]
    low[...] = values[1]
    for k in range(SUBS):
        at = slice(k * W, (k + 1) * W)
        copy(k, matrix, held, in_sems).wait()
        trailing = row * SUBS + k > panel
        values = left[at]
        factor = split(values)

        @pl.when(trailing & (col == 0))
        def _():
            edge = (panel + 1) * W
            held[at, panel * W : edge] = values
            held[at, edge:] = held[at, edge:] - dot3(factor, (high[:, edge:], low[:, edge:]))

        @pl.when(trailing & (col != 0))
        def _():
            held[at] = held[at] - dot3(factor, (high[...], low[...]))

        copy(k, held, out_hbm, out_sems).start()
    for k in range(SUBS):
        copy(k, held, out_hbm, out_sems).wait()


def update(panel, place, matrix, pieces):
    return pl.pallas_call(
        lambda *refs: update_kernel(panel, *refs),
        in_specs=[SMEM] + [ANY] * 13,
        out_specs=ANY,
        out_shape=f32(FULL, FULL),
        scratch_shapes=[
            space(FULL, W),
            space(W, FULL),
            space(W, FULL, dtype=jnp.bfloat16),
            space(W, FULL, dtype=jnp.bfloat16),
            space(FULL, FULL),
            DMA((4,)),
            DMA((SUBS,)),
            DMA((SUBS,)),
        ],
        name="update",
        **params(6 * FULL * FULL * W, 10 * FULL * FULL),
    )(place, *pieces, matrix)


def exchange(value):
    return lax.all_to_all(value, PLANE, split_axis=0, concat_axis=0, tiled=True)


def broadcast(halves, beside):
    la, lb, ra, rb = halves
    row, col = lax.axis_index("row"), lax.axis_index("col")
    la1 = lax.ppermute(la, "col", [(0, 1)])
    ra1 = lax.ppermute(ra, "row", [(0, 1)])
    lb1 = lax.ppermute(lb, "col", [(0, 3)])
    rb1 = lax.ppermute(rb, "row", [(0, 3)])
    la1, lb1, ra1, rb1, beside = lax.optimization_barrier((la1, lb1, ra1, rb1, beside))
    la2 = lax.ppermute(jnp.where(col == 1, la1, la), "col", [(0, 3), (1, 2)])
    ra2 = lax.ppermute(jnp.where(row == 1, ra1, ra), "row", [(0, 3), (1, 2)])
    lb2 = lax.ppermute(jnp.where(col == 3, lb1, lb), "col", [(0, 1), (3, 2)])
    rb2 = lax.ppermute(jnp.where(row == 3, rb1, rb), "row", [(0, 1), (3, 2)])
    return (la, la1, la2, lb, lb1, lb2, ra, ra1, ra2, rb, rb1, rb2), beside


def per_device(parent_front, child_tiles, destination, row_map, col_map, pivot_inverse):
    parent = parent_front[0]
    inverses = pivot_inverse[0]
    place = jnp.stack([lax.axis_index("row"), lax.axis_index("col")]).astype(jnp.int32)
    subs = SUBS * SUBS
    strips = exchange(permute_tiles(child_tiles, destination, row_map, col_map))
    got = exchange(reduce_strips(strips, NJ * subs).reshape(NJ, subs, STRIP, W))
    pieces, matrix = broadcast(first_panel(parent, got, inverses), assemble(parent, got))
    second = second_panel(place, pieces, matrix, inverses)
    later, matrix = broadcast(second, update(0, place, matrix, pieces))
    return update(1, place, matrix, later)[None]


def solution(mesh):
    in_specs = (
        P("front", "row", "col"),
        P(("front", "row", "col"), None, None),
        P(("front", "row", "col"), None),
        P(("front", "row", "col"), None),
        P(("front", "row", "col"), None),
        P("front", None, None, None),
    )
    out_specs = P("front", "row", "col")
    return jax.shard_map(
        per_device, mesh=mesh, in_specs=in_specs, out_specs=out_specs, check_vma=False
    )
```

time: 571 us -> 289 us (0.51)
  waiting for transfers between devices: 416 us -> 22.1 us
  blocking collectives: 0 us -> 164 us
  matrix products: 65.5 us -> 0 us
  Pallas kernels: 0 us -> 49.4 us
  local copies, waits for them, and re-layouts: 44.4 us -> 0.87 us
  starting transfers between devices: 16.1 us -> 47.9 us
  between operations: 13.3 us -> 0.42 us
  other arithmetic: 14.8 us -> 2.31 us
    all_to_all x2 -> x0, waiting for transfers between devices: 221 us -> none  [the longest x1 221 us: per_device(): lax.all_to_all(send_tiles, ('front', 'row'), split_axis=0, concat_axis=0,...]
    psum x4 -> x0, waiting for transfers between devices: 195 us -> none  [spread(): return lax.psum(kept, axis)]
    all_to_all x0 -> x2, blocking collectives: none -> 164 us  [exchange(): return lax.all_to_all(value, PLANE, split_axis=0, concat_axis=0, tiled=True)]
    dot_general x7 -> x0, matrix products: 65.5 us -> none  [the longest x1 22.4 us: permute_tiles(): jnp.einsum('...ia,...ij->...aj', row_onehot, values, precision=lax.Precis...]
    pallas_call x0 -> x7, Pallas kernels: none -> 49.4 us  [the longest x2 10.8 us: update(): pl.pallas_call(lambda *refs: update_kernel(panel, *refs), in_specs=[SMEM]...]
    ppermute x0 -> x16, starting transfers between devices: none -> 47.9 us  [the longest x2 9.83 us: broadcast(): la2 = lax.ppermute(jnp.where(col == 1, la1, la), 'col', [(0, 3), (1, 2)])]
    ppermute x0 -> x16, waiting for transfers between devices: none -> 22.1 us  [the longest x2 8.67 us: broadcast(): la2 = lax.ppermute(jnp.where(col == 1, la1, la), 'col', [(0, 3), (1, 2)])]
    scatter x2 -> x0, local copies, waits for them, and re-layouts: 19.2 us -> none  [the longest x1 15.4 us: per_device(): jnp.zeros((targets, capacity, width, width), jnp.float32).at[target, slot]]
  transfers between devices with their start and end apart: 6 -> 16, of which waited for: 5 -> 8; matrix products, arithmetic and copies ran while one was open for 6% -> 0% of each run, Pallas kernels for 0% -> 4%
where the time goes in v1:
time: 289 us; the launch traced here: 287 us
  blocking collectives  164 us (57%)
  Pallas kernels  49.4 us (17%)
  starting transfers between devices  47.9 us (17%)
  waiting for transfers between devices  22.1 us (8%)
    all_to_all x2, blocking collectives, exchange(): return lax.all_to_all(value, PLANE, split_axis=0, concat_axis=0, tiled=True)  164 us
    pallas_call x2, Pallas kernels, update(): pl.pallas_call(lambda *refs: update_kernel(panel, *refs), in_specs=[SMEM]...  10.8 us
    pallas_call x1, Pallas kernels, permute_tiles(): pl.pallas_call(permute_kernel, in_specs=[VMEM, VMEM, VMEM, ANY], out_spec...  10.8 us
    pallas_call x1, Pallas kernels, reduce_strips(): pl.pallas_call(reduce_kernel, in_specs=[ANY], out_specs=ANY, out_shape=f3...  10.6 us
    ppermute x2, starting transfers between devices, broadcast(): la2 = lax.ppermute(jnp.where(col == 1, la1, la), 'col', [(0, 3), (1, 2)])  9.83 us
    ppermute x2, waiting for transfers between devices, broadcast(): la2 = lax.ppermute(jnp.where(col == 1, la1, la), 'col', [(0, 3), (1, 2)])  8.67 us
    ppermute x2, starting transfers between devices, broadcast(): ra2 = lax.ppermute(jnp.where(row == 1, ra1, ra), 'row', [(0, 3), (1, 2)])  7.6 us
    ppermute x2, starting transfers between devices, broadcast(): lb1 = lax.ppermute(lb, 'col', [(0, 3)])  7.21 us
  transfers between devices with their start and end apart: 16, of which 8 were waited for; matrix products, arithmetic and copies ran while one was open for 0% of the time, Pallas kernels for 4%

profile of v1, /device:TPU:0, one launch (start us, length us, event | category | flops | bytes accessed | tf_op | source)
XLA Modules:
  0.0 286.9 jit_solution(16703724303370014650)
XLA Ops:
  0.0 10.8 %permute.1 = f32[32,33,8,256]{3,2,1,0:T(8,128)} custom-call(s32[1,32]{1,0:T(1,128)} %bitcast.12, s32[32,256]{1,0:T(8,128)} %rows_ref.1, s32[32,256]{1,0:T(8,128)} %cols_ref.1, f32[32,256,256]{2,1,0:T(8,128)} %tiles_hbm.1), custom_call_target="tpu_custom_call" | custom-call | flops 4294967296 | bytes 16777216 | tf_op jit(solution)/shard_map/permute/pallas_call | solution.py:128
  10.8 108.1 %all_to_all.10.strips_hbm = f32[32,33,8,256]{3,2,1,0:T(8,128)} all-to-all(f32[32,33,8,256]{3,2,1,0:T(8,128)} %permute.1), channel_id=1, replica_groups=mesh['front'=8,'row'=4,'col'=4] {'front','row'}, dimensions={0} | all-to-all | bytes 17301504 | tf_op jit(solution)/shard_map/all_to_all | solution.py:440
  118.9 10.6 %reduce.1 = f32[512,8,256]{2,1,0:T(8,128)} custom-call(f32[32,33,8,256]{3,2,1,0:T(8,128)} %all_to_all.10.strips_hbm), custom_call_target="tpu_custom_call" | custom-call | flops 2097152 | bytes 12582912 | tf_op jit(solution)/shard_map/reduce/pallas_call | solution.py:187
  129.5 55.7 %all_to_all.11.got_hbm.got_ref = f32[32,16,8,256]{3,2,1,0:T(8,128)} all-to-all(f32[32,16,8,256]{3,2,1,0:T(8,128)} %bitcast.9), channel_id=1, replica_groups=mesh['front'=8,'row'=4,'col'=4] {'front','row'}, dimensions={0} | all-to-all | bytes 8388608 | tf_op jit(solution)/shard_map/all_to_all | solution.py:440
  185.2 5.0 %first_panel.1 = (f32[512,256]{1,0:T(8,128)}, f32[512,256]{1,0:T(8,128)}, f32[256,512]{1,0:T(8,128)}, f32[256,512]{1,0:T(8,128)}) custom-call(f32[1024,1024]{1,0:T(8,128)} %bitcast.7, f32[32,16,8,256]{3,2,1,0:T(8,128)} %all_to_all.11.got_hbm.got_ref, f32[2,256,256]{2,1,0:T(8,128)} %bitcast.10), custom_call_target="tpu_custom_call" | custom-call | flops 402653184 | bytes 6291456 | tf_op jit(solution)/shard_map/first_panel/pallas_call | solution.py:245
  190.2 4.3 %collective-permute-start = (f32[512,256]{1,0:T(8,128)}, f32[512,256]{1,0:T(8,128)}, u32[]{:S(2)}, u32[]{:S(2)}) collective-permute-start(f32[512,256]{1,0:T(8,128)} %get-tuple-element.23.refs_0_.refs_1_), channel_id=1, source_target_pairs={{0,1},{4,5},{8,9},{12,13},{16,17},{20,21},{24,25},{28,29},{32,33},... | collective-permute-start | bytes 1572872 | tf_op jit(solution)/shard_map/ppermute | solution.py:446
  194.5 2.9 %collective-permute-start.1 = (f32[512,256]{1,0:T(8,128)}, f32[512,256]{1,0:T(8,128)}, u32[]{:S(2)}, u32[]{:S(2)}) collective-permute-start(f32[512,256]{1,0:T(8,128)} %get-tuple-element.24.refs_3_.refs_4_), channel_id=1, source_target_pairs={{0,3},{4,7},{8,11},{12,15},{16,19},{20,23},{24,27},{28,31},{32,35}... | collective-permute-start | bytes 1572872 | tf_op jit(solution)/shard_map/ppermute | solution.py:448
  197.4 3.0 %collective-permute-start.2 = (f32[256,512]{1,0:T(8,128)}, f32[256,512]{1,0:T(8,128)}, u32[]{:S(2)}, u32[]{:S(2)}) collective-permute-start(f32[256,512]{1,0:T(8,128)} %get-tuple-element.25.refs_6_.refs_7_), channel_id=1, source_target_pairs={{0,4},{1,5},{2,6},{3,7},{16,20},{17,21},{18,22},{19,23},{32,36},{3... | collective-permute-start | bytes 1572872 | tf_op jit(solution)/shard_map/ppermute | solution.py:447
  200.4 2.8 collective-permute-start.3
  203.2 6.3 %assemble.1.refs_12_.refs_13_ = f32[1024,1024]{1,0:T(8,128)} custom-call(f32[1024,1024]{1,0:T(8,128)} %bitcast.8, f32[32,16,8,256]{3,2,1,0:T(8,128)} %all_to_all.11.got_hbm.got_ref), custom_call_target="tpu_custom_call" | custom-call | flops 1048576 | bytes 12582912 | tf_op jit(solution)/shard_map/assemble/pallas_call | solution.py:276
  209.4 0.0 collective-permute-done.refs_1_.refs_2_
  209.4 0.0 collective-permute-done.1.refs_4_.refs_5_
  209.4 1.2 collective-permute-done.2.refs_7_.refs_8_
  210.7 2.7 collective-permute-done.3.refs_10_.refs_11_
  213.4 0.1 broadcast_select_fusion.1
  213.5 1.7 collective-permute-start.7
  215.2 0.1 broadcast_select_fusion.3
  215.3 6.3 %collective-permute-start.6 = (f32[256,512]{1,0:T(8,128)S(1)}, f32[256,512]{1,0:T(8,128)S(1)}, u32[]{:S(2)}, u32[]{:S(2)}) collective-permute-start(f32[256,512]{1,0:T(8,128)S(1)} %broadcast_select_fusion.3), channel_id=1, source_target_pairs={{0,12},{4,8},{1,13},{5,9},{2,14},{6,10},{3,15},{7,11},{16,28},{20,... | collective-permute-start | bytes 1572872 | tf_op jit(solution)/shard_map/ppermute | solution.py:452
  221.6 0.1 broadcast_select_fusion.5
  221.7 1.3 collective-permute-start.5
  223.0 0.1 broadcast_select_fusion.7
  223.1 3.2 %collective-permute-start.4 = (f32[512,256]{1,0:T(8,128)S(1)}, f32[512,256]{1,0:T(8,128)}, u32[]{:S(2)}, u32[]{:S(2)}) collective-permute-start(f32[512,256]{1,0:T(8,128)S(1)} %broadcast_select_fusion.7), channel_id=1, source_target_pairs={{0,3},{1,2},{4,7},{5,6},{8,11},{9,10},{12,15},{13,14},{16,19},{17,... | collective-permute-start | bytes 1572872 | tf_op jit(solution)/shard_map/ppermute | solution.py:451
  226.3 0.6 pad_add_fusion.place_ref.refs_0_
  226.9 0.0 collective-permute-done.7.refs_11_.refs_12_
  226.9 4.5 %collective-permute-done.6.refs_8_.refs_9_ = f32[256,512]{1,0:T(8,128)S(1)} collective-permute-done((f32[256,512]{1,0:T(8,128)S(1)}, f32[256,512]{1,0:T(8,128)S(1)}, u32[]{:S(2)}, u32[]{:S(2)}) %collective-permute-start.6) | collective-permute-done | bytes 524320 | tf_op jit(solution)/shard_map/ppermute | solution.py:452
  231.4 1.4 collective-permute-done.5.refs_5_.refs_6_
  232.8 2.2 collective-permute-done.4.refs_2_.refs_3_
  235.0 6.0 %second_panel.1 = (f32[512,256]{1,0:T(8,128)}, f32[512,256]{1,0:T(8,128)}, f32[256,512]{1,0:T(8,128)}, f32[256,512]{1,0:T(8,128)}) custom-call(s32[2]{0:T(128)} %pad_add_fusion.place_ref.refs_0_, f32[512,256]{1,0:T(8,128)} %get-tuple-element.23.refs_0_.refs_1_, f32[512,256]{1,0:T(8,128)} %collective-permute-done.refs_1_.refs_2_, ...), custom_call_target="tpu_custom_call" | custom-call | flops 1207959552 | bytes 8388608 | tf_op jit(solution)/shard_map/second_panel/pallas_call | solution.py:361
  241.0 2.1 collective-permute-start.10
  243.1 2.5 collective-permute-start.11
  245.6 2.2 collective-permute-start.8
  247.8 4.3 %collective-permute-start.9 = (f32[512,256]{1,0:T(8,128)}, f32[512,256]{1,0:T(8,128)}, u32[]{:S(2)}, u32[]{:S(2)}) collective-permute-start(f32[512,256]{1,0:T(8,128)} %get-tuple-element.33.refs_4_), channel_id=1, source_target_pairs={{0,3},{4,7},{8,11},{12,15},{16,19},{20,23},{24,27},{28,31},{32,35}... | collective-permute-start | bytes 1572872 | tf_op jit(solution)/shard_map/ppermute | solution.py:448
  252.1 5.7 %update.2.refs_13_ = f32[1024,1024]{1,0:T(8,128)} custom-call(s32[2]{0:T(128)} %pad_add_fusion.place_ref.refs_0_, f32[512,256]{1,0:T(8,128)} %get-tuple-element.23.refs_0_.refs_1_, f32[512,256]{1,0:T(8,128)} %collective-permute-done.refs_1_.refs_2_, f32[512,256]{1,0:T(8,128)} %collective-permute-done.4.refs_2_.refs_3_, ...), custom_call_target="tpu_custom_call" | custom-call | flops 1610612736 | bytes 10485760 | tf_op jit(solution)/shard_map/update/pallas_call | solution.py:419
  257.8 0.0 collective-permute-done.10.refs_8_
  257.9 2.4 collective-permute-done.9.refs_5_
  260.3 1.1 broadcast_select_fusion
  261.4 2.1 collective-permute-start.15
  263.5 0.1 broadcast_select_fusion.2
  263.6 1.3 collective-permute-start.14
  264.9 0.1 broadcast_select_fusion.4
  265.0 1.3 collective-permute-start.13
  266.4 0.1 broadcast_select_fusion.6
  266.5 6.7 %collective-permute-start.12 = (f32[512,256]{1,0:T(8,128)S(1)}, f32[512,256]{1,0:T(8,128)S(1)}, u32[]{:S(2)}, u32[]{:S(2)}) collective-permute-start(f32[512,256]{1,0:T(8,128)S(1)} %broadcast_select_fusion.6), channel_id=1, source_target_pairs={{0,3},{1,2},{4,7},{5,6},{8,11},{9,10},{12,15},{13,14},{16,19},{17,... | collective-permute-start | bytes 1572872 | tf_op jit(solution)/shard_map/ppermute | solution.py:451
  273.1 0.0 collective-permute-done.15.refs_12_
  273.2 1.2 collective-permute-done.13.refs_6_
  274.4 6.5 %collective-permute-done.12.refs_3_ = f32[512,256]{1,0:T(8,128)S(1)} collective-permute-done((f32[512,256]{1,0:T(8,128)S(1)}, f32[512,256]{1,0:T(8,128)S(1)}, u32[]{:S(2)}, u32[]{:S(2)}) %collective-permute-start.12) | collective-permute-done | bytes 524320 | tf_op jit(solution)/shard_map/ppermute | solution.py:451
  280.8 0.8 copy-done.12
  281.7 5.1 %update.3 = f32[1024,1024]{1,0:T(8,128)} custom-call(s32[2]{0:T(128)} %pad_add_fusion.place_ref.refs_0_, f32[512,256]{1,0:T(8,128)} %get-tuple-element.32.refs_1_, f32[512,256]{1,0:T(8,128)} %collective-permute-done.8.refs_2_, f32[512,256]{1,0:T(8,128)} %copy-done.12, f32[512,256]{1,0:T(8,128)} %get-tuple-element.33.refs_4_, ...), custom_call_target="tpu_custom_call" | custom-call | flops 1610612736 | bytes 10485760 | tf_op jit(solution)/shard_map/update/pallas_call | solution.py:419
  (28 shorter events, 0.1 us)
Async XLA Ops:
  190.2 19.2 %collective-permute-start = (f32[512,256]{1,0:T(8,128)}, f32[512,256]{1,0:T(8,128)}, u32[]{:S(2)}, u32[]{:S(2)}) collective-permute-start(f32[512,256]{1,0:T(8,128)} %get-tuple-element.23.refs_0_.refs_1_), channel_id=1, source_target_pairs={{0,1},{4,5},{8,9},{12,13},{16,17},{20,21},{24,25},{28,29},{32,33},... | collective-permute-start | bytes 1572872 | tf_op jit(solution)/shard_map/ppermute | solution.py:446
  194.5 14.9 %collective-permute-start.1 = (f32[512,256]{1,0:T(8,128)}, f32[512,256]{1,0:T(8,128)}, u32[]{:S(2)}, u32[]{:S(2)}) collective-permute-start(f32[512,256]{1,0:T(8,128)} %get-tuple-element.24.refs_3_.refs_4_), channel_id=1, source_target_pairs={{0,3},{4,7},{8,11},{12,15},{16,19},{20,23},{24,27},{28,31},{32,35}... | collective-permute-start | bytes 1572872 | tf_op jit(solution)/shard_map/ppermute | solution.py:448
  197.4 13.2 %collective-permute-start.2 = (f32[256,512]{1,0:T(8,128)}, f32[256,512]{1,0:T(8,128)}, u32[]{:S(2)}, u32[]{:S(2)}) collective-permute-start(f32[256,512]{1,0:T(8,128)} %get-tuple-element.25.refs_6_.refs_7_), channel_id=1, source_target_pairs={{0,4},{1,5},{2,6},{3,7},{16,20},{17,21},{18,22},{19,23},{32,36},{3... | collective-permute-start | bytes 1572872 | tf_op jit(solution)/shard_map/ppermute | solution.py:447
  200.4 13.0 %collective-permute-start.3 = (f32[256,512]{1,0:T(8,128)}, f32[256,512]{1,0:T(8,128)}, u32[]{:S(2)}, u32[]{:S(2)}) collective-permute-start(f32[256,512]{1,0:T(8,128)} %get-tuple-element.26.refs_9_.refs_10_), channel_id=1, source_target_pairs={{0,12},{1,13},{2,14},{3,15},{16,28},{17,29},{18,30},{19,31},{32,44... | collective-permute-start | bytes 1572872 | tf_op jit(solution)/shard_map/ppermute | solution.py:449
  203.1 10.2 %copy-start.3 = (f32[256,512]{1,0:T(8,128)S(1)}, f32[256,512]{1,0:T(8,128)}, u32[]{:S(2)}) copy-start(f32[256,512]{1,0:T(8,128)} %get-tuple-element.26.refs_9_.refs_10_) | copy-start | bytes 1572868
  203.1 12.0 %copy-start.2 = (f32[256,512]{1,0:T(8,128)S(1)}, f32[256,512]{1,0:T(8,128)}, u32[]{:S(2)}) copy-start(f32[256,512]{1,0:T(8,128)} %get-tuple-element.25.refs_6_.refs_7_) | copy-start | bytes 1572868
  203.2 18.4 %copy-start.1 = (f32[512,256]{1,0:T(8,128)S(1)}, f32[512,256]{1,0:T(8,128)}, u32[]{:S(2)}) copy-start(f32[512,256]{1,0:T(8,128)} %get-tuple-element.24.refs_3_.refs_4_) | copy-start | bytes 1572868
  209.4 13.6 %copy-start = (f32[512,256]{1,0:T(8,128)S(1)}, f32[512,256]{1,0:T(8,128)}, u32[]{:S(2)}) copy-start(f32[512,256]{1,0:T(8,128)} %get-tuple-element.23.refs_0_.refs_1_) | copy-start | bytes 1572868
  213.5 13.4 %collective-permute-start.7 = (f32[256,512]{1,0:T(8,128)S(1)}, f32[256,512]{1,0:T(8,128)S(1)}, u32[]{:S(2)}, u32[]{:S(2)}) collective-permute-start(f32[256,512]{1,0:T(8,128)S(1)} %broadcast_select_fusion.1), channel_id=1, source_target_pairs={{0,4},{12,8},{1,5},{13,9},{2,6},{14,10},{3,7},{15,11},{16,20},{28,... | collective-permute-start | bytes 1572872 | tf_op jit(solution)/shard_map/ppermute | solution.py:454
  215.3 16.1 %collective-permute-start.6 = (f32[256,512]{1,0:T(8,128)S(1)}, f32[256,512]{1,0:T(8,128)S(1)}, u32[]{:S(2)}, u32[]{:S(2)}) collective-permute-start(f32[256,512]{1,0:T(8,128)S(1)} %broadcast_select_fusion.3), channel_id=1, source_target_pairs={{0,12},{4,8},{1,13},{5,9},{2,14},{6,10},{3,15},{7,11},{16,28},{20,... | collective-permute-start | bytes 1572872 | tf_op jit(solution)/shard_map/ppermute | solution.py:452
  221.7 11.1 %collective-permute-start.5 = (f32[512,256]{1,0:T(8,128)S(1)}, f32[512,256]{1,0:T(8,128)S(1)}, u32[]{:S(2)}, u32[]{:S(2)}) collective-permute-start(f32[512,256]{1,0:T(8,128)S(1)} %broadcast_select_fusion.5), channel_id=1, source_target_pairs={{0,1},{3,2},{4,5},{7,6},{8,9},{11,10},{12,13},{15,14},{16,17},{19,... | collective-permute-start | bytes 1572872 | tf_op jit(solution)/shard_map/ppermute | solution.py:453
  223.1 11.9 %collective-permute-start.4 = (f32[512,256]{1,0:T(8,128)S(1)}, f32[512,256]{1,0:T(8,128)}, u32[]{:S(2)}, u32[]{:S(2)}) collective-permute-start(f32[512,256]{1,0:T(8,128)S(1)} %broadcast_select_fusion.7), channel_id=1, source_target_pairs={{0,3},{1,2},{4,7},{5,6},{8,11},{9,10},{12,15},{13,14},{16,19},{17,... | collective-permute-start | bytes 1572872 | tf_op jit(solution)/shard_map/ppermute | solution.py:451
  226.9 8.1 %copy-start.4 = (f32[256,512]{1,0:T(8,128)}, f32[256,512]{1,0:T(8,128)S(1)}, u32[]{:S(2)}) copy-start(f32[256,512]{1,0:T(8,128)S(1)} %collective-permute-done.7.refs_11_.refs_12_) | copy-start | bytes 1572868
  231.4 3.6 %copy-start.5 = (f32[256,512]{1,0:T(8,128)}, f32[256,512]{1,0:T(8,128)S(1)}, u32[]{:S(2)}) copy-start(f32[256,512]{1,0:T(8,128)S(1)} %collective-permute-done.6.refs_8_.refs_9_) | copy-start | bytes 1572868
  232.8 2.2 copy-start.6
  241.0 16.9 %collective-permute-start.10 = (f32[256,512]{1,0:T(8,128)}, f32[256,512]{1,0:T(8,128)}, u32[]{:S(2)}, u32[]{:S(2)}) collective-permute-start(f32[256,512]{1,0:T(8,128)} %get-tuple-element.34.refs_7_), channel_id=1, source_target_pairs={{0,4},{1,5},{2,6},{3,7},{16,20},{17,21},{18,22},{19,23},{32,36},{3... | collective-permute-start | bytes 1572872 | tf_op jit(solution)/shard_map/ppermute | solution.py:447
  243.1 14.8 %collective-permute-start.11 = (f32[256,512]{1,0:T(8,128)}, f32[256,512]{1,0:T(8,128)}, u32[]{:S(2)}, u32[]{:S(2)}) collective-permute-start(f32[256,512]{1,0:T(8,128)} %get-tuple-element.35.refs_10_), channel_id=1, source_target_pairs={{0,12},{1,13},{2,14},{3,15},{16,28},{17,29},{18,30},{19,31},{32,44... | collective-permute-start | bytes 1572872 | tf_op jit(solution)/shard_map/ppermute | solution.py:449
  245.6 12.3 %collective-permute-start.8 = (f32[512,256]{1,0:T(8,128)}, f32[512,256]{1,0:T(8,128)}, u32[]{:S(2)}, u32[]{:S(2)}) collective-permute-start(f32[512,256]{1,0:T(8,128)} %get-tuple-element.32.refs_1_), channel_id=1, source_target_pairs={{0,1},{4,5},{8,9},{12,13},{16,17},{20,21},{24,25},{28,29},{32,33},... | collective-permute-start | bytes 1572872 | tf_op jit(solution)/shard_map/ppermute | solution.py:446
  247.8 15.7 %copy-start.9 = (f32[256,512]{1,0:T(8,128)S(1)}, f32[256,512]{1,0:T(8,128)}, u32[]{:S(2)}) copy-start(f32[256,512]{1,0:T(8,128)} %get-tuple-element.34.refs_7_) | copy-start | bytes 1572868
  247.8 17.2 %copy-start.8 = (f32[512,256]{1,0:T(8,128)S(1)}, f32[512,256]{1,0:T(8,128)}, u32[]{:S(2)}) copy-start(f32[512,256]{1,0:T(8,128)} %get-tuple-element.33.refs_4_) | copy-start | bytes 1572868
  247.8 12.5 %collective-permute-start.9 = (f32[512,256]{1,0:T(8,128)}, f32[512,256]{1,0:T(8,128)}, u32[]{:S(2)}, u32[]{:S(2)}) collective-permute-start(f32[512,256]{1,0:T(8,128)} %get-tuple-element.33.refs_4_), channel_id=1, source_target_pairs={{0,3},{4,7},{8,11},{12,15},{16,19},{20,23},{24,27},{28,31},{32,35}... | collective-permute-start | bytes 1572872 | tf_op jit(solution)/shard_map/ppermute | solution.py:448
  257.8 8.5 %copy-start.7 = (f32[512,256]{1,0:T(8,128)S(1)}, f32[512,256]{1,0:T(8,128)}, u32[]{:S(2)}) copy-start(f32[512,256]{1,0:T(8,128)} %get-tuple-element.32.refs_1_) | copy-start | bytes 1572868
  261.4 11.7 %collective-permute-start.15 = (f32[256,512]{1,0:T(8,128)S(1)}, f32[256,512]{1,0:T(8,128)}, u32[]{:S(2)}, u32[]{:S(2)}) collective-permute-start(f32[256,512]{1,0:T(8,128)S(1)} %broadcast_select_fusion), channel_id=1, source_target_pairs={{0,4},{12,8},{1,5},{13,9},{2,6},{14,10},{3,7},{15,11},{16,20},{28,... | collective-permute-start | bytes 1572872 | tf_op jit(solution)/shard_map/ppermute | solution.py:454
  263.6 9.5 %collective-permute-start.14 = (f32[256,512]{1,0:T(8,128)S(1)}, f32[256,512]{1,0:T(8,128)S(1)}, u32[]{:S(2)}, u32[]{:S(2)}) collective-permute-start(f32[256,512]{1,0:T(8,128)S(1)} %broadcast_select_fusion.2), channel_id=1, source_target_pairs={{0,12},{4,8},{1,13},{5,9},{2,14},{6,10},{3,15},{7,11},{16,28},{20,... | collective-permute-start | bytes 1572872 | tf_op jit(solution)/shard_map/ppermute | solution.py:452
  265.0 9.3 %collective-permute-start.13 = (f32[512,256]{1,0:T(8,128)S(1)}, f32[512,256]{1,0:T(8,128)S(1)}, u32[]{:S(2)}, u32[]{:S(2)}) collective-permute-start(f32[512,256]{1,0:T(8,128)S(1)} %broadcast_select_fusion.4), channel_id=1, source_target_pairs={{0,1},{3,2},{4,5},{7,6},{8,9},{11,10},{12,13},{15,14},{16,17},{19,... | collective-permute-start | bytes 1572872 | tf_op jit(solution)/shard_map/ppermute | solution.py:453
  266.5 14.4 %collective-permute-start.12 = (f32[512,256]{1,0:T(8,128)S(1)}, f32[512,256]{1,0:T(8,128)S(1)}, u32[]{:S(2)}, u32[]{:S(2)}) collective-permute-start(f32[512,256]{1,0:T(8,128)S(1)} %broadcast_select_fusion.6), channel_id=1, source_target_pairs={{0,3},{1,2},{4,7},{5,6},{8,11},{9,10},{12,15},{13,14},{16,19},{17,... | collective-permute-start | bytes 1572872 | tf_op jit(solution)/shard_map/ppermute | solution.py:451
  273.1 7.7 %copy-start.10 = (f32[256,512]{1,0:T(8,128)}, f32[256,512]{1,0:T(8,128)S(1)}, u32[]{:S(2)}) copy-start(f32[256,512]{1,0:T(8,128)S(1)} %collective-permute-done.14.refs_9_) | copy-start | bytes 1572868
  274.4 6.5 %copy-start.11 = (f32[512,256]{1,0:T(8,128)}, f32[512,256]{1,0:T(8,128)S(1)}, u32[]{:S(2)}) copy-start(f32[512,256]{1,0:T(8,128)S(1)} %collective-permute-done.13.refs_6_) | copy-start | bytes 1572868
  280.8 0.8 copy-start.12

commit v2 on v0

v2 whole, which is shorter than its diff:
```python
import jax
import jax.numpy as jnp
from jax import lax
from jax.experimental import pallas as pl
from jax.experimental.pallas import tpu as pltpu
from jax.sharding import PartitionSpec as P

PLANE = ("front", "row")
W = 256
SUBS = 4
FULL = SUBS * W
HALF = 2 * W
STRIP = 8
LANES = 128
NJ = 32
RING = 4
HBM = pl.BlockSpec(memory_space=pltpu.HBM)
VMEM = pl.BlockSpec(memory_space=pltpu.VMEM)
DMA = pltpu.SemaphoreType.DMA


def f32(*shape):
    return jax.ShapeDtypeStruct(shape, jnp.float32)


def space(*shape, dtype=jnp.float32):
    return pltpu.VMEM(shape, dtype)


def params(flops, moved, mib=18):
    return {
        "compiler_params": pltpu.CompilerParams(vmem_limit_bytes=mib * 1024 * 1024),
        "cost_estimate": pl.CostEstimate(flops=flops, bytes_accessed=moved, transcendentals=0),
    }


def split(value):
    high = value.astype(jnp.bfloat16)
    low = (value - high.astype(jnp.float32)).astype(jnp.bfloat16)
    return high, low


def dot(a, b):
    return jnp.dot(a, b, preferred_element_type=jnp.float32)


def dot3(a, b):
    ah, al = a
    bh, bl = b
    return dot(ah, bh) + (dot(ah, bl) + dot(al, bh))


def place_of(row, col):
    least = jnp.minimum(row, col)
    first = jnp.where(col == 0, row, 3 + col)
    second = jnp.where(col == 1, 6 + row, 8 + col)
    rest = 12 + (row - 2) * 2 + (col - 2)
    return jnp.where(least == 0, first, jnp.where(least == 1, second, rest))


PLACE = {}
for _r in range(SUBS):
    for _c in range(SUBS):
        PLACE[_r, _c] = (
            (_r if _c == 0 else 3 + _c)
            if min(_r, _c) == 0
            else (6 + _r if _c == 1 else 8 + _c)
            if min(_r, _c) == 1
            else 12 + (_r - 2) * 2 + _c - 2
        )


GROUPS = (4, 12, 12, 4)


def permute_kernel(
    dest_hbm, rows_hbm, cols_hbm, tiles_hbm, out_hbm, dest, rows, cols, tiles, out, sems, out_sems
):
    count = tiles.shape[0]
    maps = [
        pltpu.make_async_copy(rows_hbm, rows, sems.at[0]),
        pltpu.make_async_copy(cols_hbm, cols, sems.at[1]),
        pltpu.make_async_copy(dest_hbm, dest, sems.at[2]),
    ]
    loads = []
    first = 0
    for k, size in enumerate(GROUPS):
        at = pl.ds(first, size)
        loads.append(pltpu.make_async_copy(tiles_hbm.at[at], tiles.at[at], sems.at[3 + k]))
        first += size
    for copy in maps + loads:
        copy.start()
    for copy in maps:
        copy.wait()

    place = place_of(rows[:, :1] // W, cols[:, :1] // W).astype(jnp.float32)
    same = lax.broadcasted_iota(jnp.int32, (count, LANES), 0) == lax.broadcasted_iota(
        jnp.int32, (count, LANES), 1
    )
    line = jnp.sum(jnp.where(same, place, 0.0), axis=0, keepdims=True)
    out[:, 2 * count] = jnp.broadcast_to(line[None], (NJ, STRIP, LANES))
    line = line[:, :count] + (dest[...] * (SUBS * SUBS)).astype(jnp.float32)
    out[:, 2 * count, :, :count] = jnp.broadcast_to(line[None], (NJ, STRIP, count))

    index = lax.broadcasted_iota(jnp.int32, (W, W), 0)
    stores = []
    contract = (((1,), (1,)), ((), ()))
    first = 0
    for load, size in zip(loads, GROUPS):
        load.wait()
        for i in range(first, first + size):
            row_hot = (index == (rows[i : i + 1] & (W - 1))).astype(jnp.float32)
            col_hot = (index == (cols[i : i + 1] & (W - 1))).astype(jnp.float32)
            row_hot = row_hot.astype(jnp.bfloat16)
            col_hot = col_hot.astype(jnp.bfloat16)
            high, low = split(tiles[i])
            high = dot(row_hot, high).astype(jnp.bfloat16)
            low = dot(row_hot, low).astype(jnp.bfloat16)
            moved = lax.dot_general(
                jnp.concatenate([high, low], axis=1),
                jnp.concatenate([col_hot, col_hot], axis=1),
                contract,
                preferred_element_type=jnp.float32,
            )
            out[:, 2 * i] = moved[:, :LANES].reshape(NJ, STRIP, LANES)
            out[:, 2 * i + 1] = moved[:, LANES:].reshape(NJ, STRIP, LANES)
        at = pl.ds(2 * first, 2 * size + (first + size == count))
        sem = out_sems.at[len(stores)]
        stores.append(pltpu.make_async_copy(out.at[:, at], out_hbm.at[:, at], sem))
        stores[-1].start()
        first += size
    for store in stores:
        store.wait()


def permute_tiles(child_tiles, destination, row_map, col_map):
    count = child_tiles.shape[0]
    return pl.pallas_call(
        permute_kernel,
        in_specs=[HBM] * 4,
        out_specs=HBM,
        out_shape=f32(NJ, 2 * count + 1, STRIP, LANES),
        scratch_shapes=[
            space(1, count, dtype=jnp.int32),
            space(count, W, dtype=jnp.int32),
            space(count, W, dtype=jnp.int32),
            space(count, W, W),
            space(NJ, 2 * count + 1, STRIP, LANES),
            DMA((3 + len(GROUPS),)),
            DMA((len(GROUPS),)),
        ],
        name="permute",
        **params(8 * count * W**3, 8 * count * W * W, 62),
    )(destination.reshape(1, count), row_map, col_map, child_tiles)


def reduce_kernel(strips, sums, codes_vmem, codes, sem):
    count = strips.shape[1] // 2
    codes_vmem[...] = strips[:, 2 * count, 0].astype(jnp.int32)
    copy = pltpu.make_async_copy(codes_vmem, codes, sem)
    copy.start()
    sums[...] = jnp.zeros_like(sums)
    copy.wait()

    def add(source, carry):
        for k in range(count):
            code = codes[source, k]
            sums[code] = sums[code] + strips[source, 2 * k : 2 * k + 2]
        return carry

    lax.fori_loop(0, NJ, add, 0)


def reduce_strips(strips, slots):
    count = strips.shape[1] // 2
    return pl.pallas_call(
        reduce_kernel,
        in_specs=[VMEM],
        out_specs=VMEM,
        out_shape=f32(slots, 2, STRIP, LANES),
        scratch_shapes=[
            space(NJ, LANES, dtype=jnp.int32),
            pltpu.SMEM((NJ, LANES), jnp.int32),
            DMA,
        ],
        name="reduce",
        **params(NJ * count * STRIP * W, 4 * (NJ * count + slots) * STRIP * W),
    )(strips)


def block(parent, got, r, c):
    place = PLACE[r, c]
    rows, cols = slice(r * W, (r + 1) * W), c * W
    left = parent[rows, cols : cols + LANES] + got[:, place, 0].reshape(W, LANES)
    right = parent[rows, cols + LANES : cols + W] + got[:, place, 1].reshape(W, LANES)
    return jnp.concatenate([left, right], axis=1)


def first_kernel(parent, got, inv_ref, la, lb, ra, rb):
    inv = split(inv_ref[0])
    for k in range(SUBS):
        half = slice(k % 2 * W, (k % 2 + 1) * W)
        (la, lb)[k // 2][half] = dot3(split(block(parent, got, k, 0)), inv)
        (ra, rb)[k // 2][:, half] = block(parent, got, 0, k)


HALVES = [f32(HALF, W), f32(HALF, W), f32(W, HALF), f32(W, HALF)]


def first_panel(parent, got, inverses):
    return pl.pallas_call(
        first_kernel,
        in_specs=[VMEM] * 3,
        out_specs=[VMEM] * 4,
        out_shape=HALVES,
        name="first_panel",
        **params(6 * FULL * W * W, 12 * FULL * W),
    )(parent, got, inverses)


def assemble_kernel(parent, got, matrix):
    for r in range(SUBS):
        for c in range(SUBS):
            rows, cols = slice(r * W, (r + 1) * W), slice(c * W, (c + 1) * W)
            matrix[rows, cols] = block(parent, got, r, c)


def assemble(parent, got):
    return pl.pallas_call(
        assemble_kernel,
        in_specs=[VMEM] * 2,
        out_specs=VMEM,
        out_shape=f32(FULL, FULL),
        name="assemble",
        **params(FULL * FULL, 12 * FULL * FULL),
    )(parent, got)


def choose(index, near, parts, target):
    own, first, second = parts

    @pl.when(index == 0)
    def _():
        target[...] = own[...]

    @pl.when(index == near)
    def _():
        target[...] = first[...]

    @pl.when((index != 0) & (index != near))
    def _():
        target[...] = second[...]


def choose_all(row, col, pieces, left, right):
    choose(col, 1, pieces[0:3], left.at[pl.ds(0, HALF)])
    choose(col, 3, pieces[3:6], left.at[pl.ds(HALF, HALF)])
    choose(row, 1, pieces[6:9], right.at[:, pl.ds(0, HALF)])
    choose(row, 3, pieces[9:12], right.at[:, pl.ds(HALF, HALF)])


def second_kernel(*refs):
    pieces = refs[:12]
    matrix, inv_ref, la, lb, ra, rb, left, right = refs[12:]
    row, col = lax.axis_index("row"), lax.axis_index("col")

    @pl.when((row == 0) | (col == 0))
    def _():
        choose_all(row, col, pieces, left, right)

    @pl.when(col == 0)
    def _():
        inv = split(inv_ref[1])
        corner = split(right[:, W:HALF])
        for k in range(SUBS):
            at = slice(k * W, (k + 1) * W)
            half = slice(k % 2 * W, (k % 2 + 1) * W)
            reduced = matrix[at, W:HALF] - dot3(split(left[at]), corner)
            (la, lb)[k // 2][half] = dot3(split(reduced), inv)

    @pl.when(row == 0)
    def _():
        below = split(left[W:HALF])
        for k in range(SUBS):
            at = slice(k * W, (k + 1) * W)
            half = slice(k % 2 * W, (k % 2 + 1) * W)
            (ra, rb)[k // 2][:, half] = matrix[W:HALF, at] - dot3(below, split(right[:, at]))


def second_panel(pieces, matrix, inverses):
    return pl.pallas_call(
        second_kernel,
        in_specs=[VMEM] * 14,
        out_specs=[VMEM] * 4,
        out_shape=HALVES,
        scratch_shapes=[space(FULL, W), space(W, FULL)],
        name="second_panel",
        **params(18 * FULL * W * W, 32 * FULL * W),
    )(*pieces, matrix, inverses)


def update_rows(panel, k, matrix, out, left, high, low):
    row, col = lax.axis_index("row"), lax.axis_index("col")
    at = slice(k * W, (k + 1) * W)
    edge = (panel + 1) * W
    trailing = row * SUBS + k > panel
    values = left[at]
    factor = split(values)

    @pl.when(jnp.logical_not(trailing))
    def _():
        out[at] = matrix[at]

    @pl.when(trailing & (col == 0))
    def _():
        if panel:
            out[at, : panel * W] = matrix[at, : panel * W]
        out[at, panel * W : edge] = values
        out[at, edge:] = matrix[at, edge:] - dot3(factor, (high[:, edge:], low[:, edge:]))

    @pl.when(trailing & (col != 0))
    def _():
        out[at] = matrix[at] - dot3(factor, (high[...], low[...]))


def prepare(pieces, left, right, high, low):
    choose_all(lax.axis_index("row"), lax.axis_index("col"), pieces, left, right)
    values = split(right[...])
    high[...] = values[0]
    low[...] = values[1]


def update_kernel(*refs):
    matrix, out, left, right, high, low = refs[12:]
    prepare(refs[:12], left, right, high, low)
    for k in range(SUBS):
        update_rows(0, k, matrix, out, left, high, low)


def finish_kernel(*refs):
    matrix, out_hbm, left, right, high, low, out, sems = refs[12:]
    prepare(refs[:12], left, right, high, low)
    stores = []
    for k in range(SUBS):
        update_rows(1, k, matrix, out, left, high, low)
        at = pl.ds(k * W, W)
        stores.append(pltpu.make_async_copy(out.at[at], out_hbm.at[at], sems.at[k]))
        stores[k].start()
    for store in stores:
        store.wait()


SCRATCH = [
    space(FULL, W),
    space(W, FULL),
    space(W, FULL, dtype=jnp.bfloat16),
    space(W, FULL, dtype=jnp.bfloat16),
]


def update(matrix, pieces):
    return pl.pallas_call(
        update_kernel,
        in_specs=[VMEM] * 13,
        out_specs=VMEM,
        out_shape=f32(FULL, FULL),
        scratch_shapes=SCRATCH,
        name="update",
        **params(6 * FULL * FULL * W, 10 * FULL * FULL),
    )(*pieces, matrix)


def finish(matrix, pieces):
    return pl.pallas_call(
        finish_kernel,
        in_specs=[VMEM] * 13,
        out_specs=HBM,
        out_shape=f32(FULL, FULL),
        scratch_shapes=SCRATCH + [space(FULL, FULL), DMA((SUBS,))],
        name="finish",
        **params(6 * FULL * FULL * W, 10 * FULL * FULL),
    )(*pieces, matrix)


def exchange(value):
    return lax.all_to_all(value, PLANE, split_axis=0, concat_axis=0, tiled=True)


RIGHT = [(k, (k + 1) % RING) for k in range(RING)]
LEFT = [(k, (k - 1) % RING) for k in range(RING)]
PAIRS = [(0, 1), (1, 0), (2, 3), (3, 2)]
CROSS = [(0, 3), (3, 0), (1, 2), (2, 1)]


def broadcast(halves, beside=()):
    la, lb, ra, rb = halves
    row, col = lax.axis_index("row"), lax.axis_index("col")
    la1 = lax.ppermute(la, "col", RIGHT)
    lb1 = lax.ppermute(lb, "col", LEFT)
    ra1 = lax.ppermute(ra, "row", RIGHT)
    rb1 = lax.ppermute(rb, "row", LEFT)
    la1, lb1 = lax.optimization_barrier((la1, lb1))
    ra1, rb1, beside = lax.optimization_barrier((ra1, rb1, beside))
    la2 = lax.ppermute(jnp.where(col == 1, la1, la), "col", CROSS)
    ra2 = lax.ppermute(jnp.where(row == 1, ra1, ra), "row", CROSS)
    lb2 = lax.ppermute(jnp.where(col == 3, lb1, lb), "col", PAIRS)
    rb2 = lax.ppermute(jnp.where(row == 3, rb1, rb), "row", PAIRS)
    return (la, la1, la2, lb, lb1, lb2, ra, ra1, ra2, rb, rb1, rb2), beside


def per_device(parent_front, child_tiles, destination, row_map, col_map, pivot_inverse):
    parent = parent_front[0]
    inverses = pivot_inverse[0]
    subs = SUBS * SUBS
    strips = exchange(permute_tiles(child_tiles, destination, row_map, col_map))
    got = exchange(reduce_strips(strips, NJ * subs).reshape(NJ, subs, 2, STRIP, LANES))
    pieces, matrix = broadcast(first_panel(parent, got, inverses), assemble(parent, got))
    second = second_panel(pieces, matrix, inverses)
    later, matrix = broadcast(second, update(matrix, pieces))
    return finish(matrix, later)[None]


def solution(mesh):
    in_specs = (
        P("front", "row", "col"),
        P(("front", "row", "col"), None, None),
        P(("front", "row", "col"), None),
        P(("front", "row", "col"), None),
        P(("front", "row", "col"), None),
        P("front", None, None, None),
    )
    out_specs = P("front", "row", "col")
    return jax.shard_map(
        per_device, mesh=mesh, in_specs=in_specs, out_specs=out_specs, check_vma=False
    )
```

time: 571 us -> 239 us (0.42)
  waiting for transfers between devices: 416 us -> 24.3 us
  blocking collectives: 0 us -> 161 us
  matrix products: 65.5 us -> 0 us
  local copies, waits for them, and re-layouts: 44.4 us -> 5.71 us
  Pallas kernels: 0 us -> 19.8 us
  other arithmetic: 14.8 us -> 0.59 us
  between operations: 13.3 us -> 0.31 us
  starting transfers between devices: 16.1 us -> 26.5 us
    all_to_all x2 -> x0, waiting for transfers between devices: 221 us -> none  [the longest x1 221 us: per_device(): lax.all_to_all(send_tiles, ('front', 'row'), split_axis=0, concat_axis=0,...]
    psum x4 -> x0, waiting for transfers between devices: 195 us -> none  [spread(): return lax.psum(kept, axis)]
    all_to_all x0 -> x2, blocking collectives: none -> 161 us  [exchange(): return lax.all_to_all(value, PLANE, split_axis=0, concat_axis=0, tiled=True)]
    dot_general x7 -> x0, matrix products: 65.5 us -> none  [the longest x1 22.4 us: permute_tiles(): jnp.einsum('...ia,...ij->...aj', row_onehot, values, precision=lax.Precis...]
    ppermute x0 -> x16, starting transfers between devices: none -> 26.5 us  [the longest x2 6.08 us: broadcast(): ra2 = lax.ppermute(jnp.where(row == 1, ra1, ra), 'row', CROSS)]
    ppermute x0 -> x16, waiting for transfers between devices: none -> 24.3 us  [the longest x2 8.46 us: broadcast(): rb2 = lax.ppermute(jnp.where(row == 3, rb1, rb), 'row', PAIRS)]
    pallas_call x0 -> x7, Pallas kernels: none -> 19.8 us  [the longest x1 8.35 us: permute_tiles(): pl.pallas_call(permute_kernel, in_specs=[HBM] * 4, out_specs=HBM, out_sha...]
    scatter x2 -> x0, local copies, waits for them, and re-layouts: 19.2 us -> none  [the longest x1 15.4 us: per_device(): jnp.zeros((targets, capacity, width, width), jnp.float32).at[target, slot]]
  transfers between devices with their start and end apart: 6 -> 16, of which waited for: 5 -> 10; matrix products, arithmetic and copies ran while one was open for 6% -> 0% of each run, Pallas kernels for 0% -> 1%
where the time goes in v2:
time: 239 us
  blocking collectives  161 us (67%)
  starting transfers between devices  26.5 us (11%)
  waiting for transfers between devices  24.3 us (10%)
  Pallas kernels  19.8 us (8%)
  local copies, waits for them, and re-layouts  5.71 us (2%)
    all_to_all x2, blocking collectives, exchange(): return lax.all_to_all(value, PLANE, split_axis=0, concat_axis=0, tiled=True)  161 us
    ppermute x2, waiting for transfers between devices, broadcast(): rb2 = lax.ppermute(jnp.where(row == 3, rb1, rb), 'row', PAIRS)  8.46 us
    pallas_call x1, Pallas kernels, permute_tiles(): pl.pallas_call(permute_kernel, in_specs=[HBM] * 4, out_specs=HBM, out_sha...  8.35 us
    ppermute x2, waiting for transfers between devices, broadcast(): ra1 = lax.ppermute(ra, 'row', RIGHT)  6.25 us
    ppermute x2, starting transfers between devices, broadcast(): ra2 = lax.ppermute(jnp.where(row == 1, ra1, ra), 'row', CROSS)  6.08 us
    unnamed x12, local copies, waits for them, and re-layouts  5.71 us
    ppermute x2, starting transfers between devices, broadcast(): rb1 = lax.ppermute(rb, 'row', LEFT)  5.7 us
    ppermute x2, starting transfers between devices, broadcast(): la2 = lax.ppermute(jnp.where(col == 1, la1, la), 'col', CROSS)  5.25 us
  transfers between devices with their start and end apart: 16, of which 10 were waited for; matrix products, arithmetic and copies ran while one was open for 0% of the time, Pallas kernels for 1%

profile of v2, /device:TPU:0, one launch (start us, length us, event | category | flops | bytes accessed | tf_op | source)
XLA Modules:
  0.0 238.6 jit_solution(6505013642120194732)
XLA Ops:
  0.0 8.3 %permute.1 = f32[32,65,8,128]{3,2,1,0:T(8,128)} custom-call(s32[1,32]{1,0:T(1,128)} %bitcast.10, s32[32,256]{1,0:T(8,128)} %rows_hbm.1, s32[32,256]{1,0:T(8,128)} %cols_hbm.1, f32[32,256,256]{2,1,0:T(8,128)} %tiles_hbm.1), custom_call_target="tpu_custom_call" | custom-call | flops 4294967296 | bytes 16777216 | tf_op jit(solution)/shard_map/permute/pallas_call | solution.py:138
  8.4 106.7 %all_to_all.10.strips = f32[32,65,8,128]{3,2,1,0:T(8,128)S(1)} all-to-all(f32[32,65,8,128]{3,2,1,0:T(8,128)} %permute.1), channel_id=1, replica_groups=mesh['front'=8,'row'=4,'col'=4] {'front','row'}, dimensions={0} | all-to-all | bytes 17039360 | tf_op jit(solution)/shard_map/all_to_all | solution.py:386
  115.0 3.6 %reduce.1 = f32[512,2,8,128]{3,2,1,0:T(8,128)S(1)} custom-call(f32[32,65,8,128]{3,2,1,0:T(8,128)S(1)} %all_to_all.10.strips), custom_call_target="tpu_custom_call" | custom-call | flops 2097152 | bytes 12582912 | tf_op jit(solution)/shard_map/reduce/pallas_call | solution.py:176
  118.6 0.0 copy-start.2
  118.6 0.0 copy-start.4
  118.6 54.7 %all_to_all.11.got = f32[32,16,2,8,128]{4,3,2,1,0:T(8,128)S(1)} all-to-all(f32[32,16,2,8,128]{4,3,2,1,0:T(8,128)S(1)} %bitcast.7), channel_id=1, replica_groups=mesh['front'=8,'row'=4,'col'=4] {'front','row'}, dimensions={0} | all-to-all | bytes 8388608 | tf_op jit(solution)/shard_map/all_to_all | solution.py:386
  173.3 0.7 first_panel.1
  174.0 1.3 copy-done
  175.3 0.2 collective-permute-start.4
  175.5 3.0 %collective-permute-start.5 = (f32[256,512]{1,0:T(8,128)S(1)}, f32[256,512]{1,0:T(8,128)S(1)}, u32[]{:S(2)}, u32[]{:S(2)}) collective-permute-start(f32[256,512]{1,0:T(8,128)S(1)} %get-tuple-element.28.refs_9_), channel_id=1, source_target_pairs={{0,12},{4,0},{8,4},{12,8},{1,13},{5,1},{9,5},{13,9},{2,14},{6,2},{... | collective-permute-start | bytes 1572872 | tf_op jit(solution)/shard_map/ppermute | solution.py:401
  178.5 1.6 collective-permute-start
  180.1 1.7 collective-permute-start.1
  181.8 2.2 copy-done.1
  184.0 2.2 copy-done.3
  186.2 0.5 assemble.1.refs_12_
  186.7 0.0 copy-start.5
  186.7 3.1 %collective-permute-done.4.refs_7_ = f32[256,512]{1,0:T(8,128)S(1)} collective-permute-done((f32[256,512]{1,0:T(8,128)S(1)}, f32[256,512]{1,0:T(8,128)S(1)}, u32[]{:S(2)}, u32[]{:S(2)}) %collective-permute-start.4) | collective-permute-done | bytes 524320 | tf_op jit(solution)/shard_map/ppermute | solution.py:400
  189.8 0.1 broadcast_select_fusion.1
  189.9 0.3 collective-permute-start.7
  190.2 0.1 broadcast_select_fusion.3
  190.3 2.8 %collective-permute-start.6 = (f32[256,512]{1,0:T(8,128)S(1)}, f32[256,512]{1,0:T(8,128)S(1)}, u32[]{:S(2)}, u32[]{:S(2)}) collective-permute-start(f32[256,512]{1,0:T(8,128)S(1)} %broadcast_select_fusion.3), channel_id=1, source_target_pairs={{0,12},{12,0},{4,8},{8,4},{1,13},{13,1},{5,9},{9,5},{2,14},{14,2},... | collective-permute-start | bytes 1572872 | tf_op jit(solution)/shard_map/ppermute | solution.py:405
  193.1 0.1 broadcast_select_fusion.5
  193.2 1.7 collective-permute-start.3
  194.8 0.1 broadcast_select_fusion.7
  194.9 2.3 collective-permute-start.2
  197.1 5.1 %collective-permute-done.7.refs_11_ = f32[256,512]{1,0:T(8,128)S(1)} collective-permute-done((f32[256,512]{1,0:T(8,128)S(1)}, f32[256,512]{1,0:T(8,128)S(1)}, u32[]{:S(2)}, u32[]{:S(2)}) %collective-permute-start.7) | collective-permute-done | bytes 524320 | tf_op jit(solution)/shard_map/ppermute | solution.py:407
  202.3 1.4 collective-permute-done.6.refs_8_
  203.7 1.3 collective-permute-done.3.refs_5_
  205.0 2.7 %collective-permute-done.2.refs_2_ = f32[512,256]{1,0:T(8,128)S(1)} collective-permute-done((f32[512,256]{1,0:T(8,128)S(1)}, f32[512,256]{1,0:T(8,128)S(1)}, u32[]{:S(2)}, u32[]{:S(2)}) %collective-permute-start.2) | collective-permute-done | bytes 524320 | tf_op jit(solution)/shard_map/ppermute | solution.py:404
  207.7 2.2 second_panel.1
  209.8 0.6 collective-permute-start.12
  210.4 2.7 %collective-permute-start.13 = (f32[256,512]{1,0:T(8,128)S(1)}, f32[256,512]{1,0:T(8,128)S(1)}, u32[]{:S(2)}, u32[]{:S(2)}) collective-permute-start(f32[256,512]{1,0:T(8,128)S(1)} %get-tuple-element.37.refs_9_), channel_id=1, source_target_pairs={{0,12},{4,0},{8,4},{12,8},{1,13},{5,1},{9,5},{13,9},{2,14},{6,2},{... | collective-permute-start | bytes 1572872 | tf_op jit(solution)/shard_map/ppermute | solution.py:401
  213.1 3.2 %collective-permute-start.9 = (f32[512,256]{1,0:T(8,128)S(1)}, f32[512,256]{1,0:T(8,128)S(1)}, u32[]{:S(2)}, u32[]{:S(2)}) collective-permute-start(f32[512,256]{1,0:T(8,128)S(1)} %get-tuple-element.33.refs_3_), channel_id=1, source_target_pairs={{0,3},{1,0},{2,1},{3,2},{4,7},{5,4},{6,5},{7,6},{8,11},{9,8},{10,9... | collective-permute-start | bytes 1572872 | tf_op jit(solution)/shard_map/ppermute | solution.py:399
  216.4 2.1 update.1.refs_12_
  218.5 3.2 %collective-permute-done.12.refs_7_ = f32[256,512]{1,0:T(8,128)S(1)} collective-permute-done((f32[256,512]{1,0:T(8,128)S(1)}, f32[256,512]{1,0:T(8,128)S(1)}, u32[]{:S(2)}, u32[]{:S(2)}) %collective-permute-start.12) | collective-permute-done | bytes 524320 | tf_op jit(solution)/shard_map/ppermute | solution.py:400
  221.7 0.1 broadcast_select_fusion
  221.8 0.1 collective-permute-start.15
  221.9 0.1 broadcast_select_fusion.2
  222.0 3.3 %collective-permute-start.14 = (f32[256,512]{1,0:T(8,128)S(1)}, f32[256,512]{1,0:T(8,128)S(1)}, u32[]{:S(2)}, u32[]{:S(2)}) collective-permute-start(f32[256,512]{1,0:T(8,128)S(1)} %broadcast_select_fusion.2), channel_id=1, source_target_pairs={{0,12},{12,0},{4,8},{8,4},{1,13},{13,1},{5,9},{9,5},{2,14},{14,2},... | collective-permute-start | bytes 1572872 | tf_op jit(solution)/shard_map/ppermute | solution.py:405
  225.2 0.1 broadcast_select_fusion.4
  225.3 0.1 collective-permute-start.11
  225.4 0.1 broadcast_select_fusion.6
  225.5 3.0 %collective-permute-start.10 = (f32[512,256]{1,0:T(8,128)S(1)}, f32[512,256]{1,0:T(8,128)S(1)}, u32[]{:S(2)}, u32[]{:S(2)}) collective-permute-start(f32[512,256]{1,0:T(8,128)S(1)} %broadcast_select_fusion.6), channel_id=1, source_target_pairs={{0,3},{3,0},{1,2},{2,1},{4,7},{7,4},{5,6},{6,5},{8,11},{11,8},{9,1... | collective-permute-start | bytes 1572872 | tf_op jit(solution)/shard_map/ppermute | solution.py:404
  228.5 3.3 %collective-permute-done.15.refs_11_ = f32[256,512]{1,0:T(8,128)S(1)} collective-permute-done((f32[256,512]{1,0:T(8,128)S(1)}, f32[256,512]{1,0:T(8,128)S(1)}, u32[]{:S(2)}, u32[]{:S(2)}) %collective-permute-start.15) | collective-permute-done | bytes 524320 | tf_op jit(solution)/shard_map/ppermute | solution.py:407
  231.8 1.1 collective-permute-done.14.refs_8_
  232.9 1.6 collective-permute-done.11.refs_5_
  234.6 1.4 collective-permute-done.10.refs_2_
  236.0 2.5 %finish.1 = f32[1024,1024]{1,0:T(8,128)} custom-call(f32[512,256]{1,0:T(8,128)S(1)} %get-tuple-element.32.refs_0_, f32[512,256]{1,0:T(8,128)S(1)} %collective-permute-done.8.refs_1_, f32[512,256]{1,0:T(8,128)S(1)} %collective-permute-done.10.refs_2_, f32[512,256]{1,0:T(8,128)S(1)} %get-tuple-element.33.refs_3_, ...), custom_call_target="tpu_custom_call" | custom-call | flops 1610612736 | bytes 10485760 | tf_op jit(solution)/shard_map/finish/pallas_call | solution.py:374
  (13 shorter events, 0.0 us)
Async XLA Ops:
  118.6 54.7 %copy-start.2 = (f32[1,1024,1024]{2,1,0:T(8,128)S(1)}, f32[1,1024,1024]{2,1,0:T(8,128)}, u32[]{:S(2)}) copy-start(f32[1,1024,1024]{2,1,0:T(8,128)} %param.6) | copy-start | bytes 12582916
  118.6 54.7 %copy-start.4 = (f32[1,2,256,256]{3,2,1,0:T(8,128)S(1)}, f32[1,2,256,256]{3,2,1,0:T(8,128)}, u32[]{:S(2)}) copy-start(f32[1,2,256,256]{3,2,1,0:T(8,128)} %param.11) | copy-start | bytes 1572868
  173.3 2.0 copy-start
  175.3 14.5 %collective-permute-start.4 = (f32[256,512]{1,0:T(8,128)S(1)}, f32[256,512]{1,0:T(8,128)S(1)}, u32[]{:S(2)}, u32[]{:S(2)}) collective-permute-start(f32[256,512]{1,0:T(8,128)S(1)} %get-tuple-element.27.refs_6_), channel_id=1, source_target_pairs={{0,4},{4,8},{8,12},{12,0},{1,5},{5,9},{9,13},{13,1},{2,6},{6,10},{... | collective-permute-start | bytes 1572872 | tf_op jit(solution)/shard_map/ppermute | solution.py:400
  175.5 14.2 %collective-permute-start.5 = (f32[256,512]{1,0:T(8,128)S(1)}, f32[256,512]{1,0:T(8,128)S(1)}, u32[]{:S(2)}, u32[]{:S(2)}) collective-permute-start(f32[256,512]{1,0:T(8,128)S(1)} %get-tuple-element.28.refs_9_), channel_id=1, source_target_pairs={{0,12},{4,0},{8,4},{12,8},{1,13},{5,1},{9,5},{13,9},{2,14},{6,2},{... | collective-permute-start | bytes 1572872 | tf_op jit(solution)/shard_map/ppermute | solution.py:401
  178.5 14.5 %collective-permute-start = (f32[512,256]{1,0:T(8,128)S(1)}, f32[512,256]{1,0:T(8,128)S(1)}, u32[]{:S(2)}, u32[]{:S(2)}) collective-permute-start(f32[512,256]{1,0:T(8,128)S(1)} %get-tuple-element.23.refs_0_), channel_id=1, source_target_pairs={{0,1},{1,2},{2,3},{3,0},{4,5},{5,6},{6,7},{7,4},{8,9},{9,10},{10,1... | collective-permute-start | bytes 1572872 | tf_op jit(solution)/shard_map/ppermute | solution.py:398
  180.1 13.0 %collective-permute-start.1 = (f32[512,256]{1,0:T(8,128)S(1)}, f32[512,256]{1,0:T(8,128)S(1)}, u32[]{:S(2)}, u32[]{:S(2)}) collective-permute-start(f32[512,256]{1,0:T(8,128)S(1)} %get-tuple-element.24.refs_3_), channel_id=1, source_target_pairs={{0,3},{1,0},{2,1},{3,2},{4,7},{5,4},{6,5},{7,6},{8,11},{9,8},{10,9... | collective-permute-start | bytes 1572872 | tf_op jit(solution)/shard_map/ppermute | solution.py:399
  181.8 2.2 copy-start.1
  184.0 2.2 copy-start.3
  186.7 21.0 %copy-start.5 = (f32[1,2,256,256]{3,2,1,0:T(8,128)S(1)}, f32[1,2,256,256]{3,2,1,0:T(8,128)}, u32[]{:S(2)}) copy-start(f32[1,2,256,256]{3,2,1,0:T(8,128)} %param.11) | copy-start | bytes 1572868
  189.9 12.4 %collective-permute-start.7 = (f32[256,512]{1,0:T(8,128)S(1)}, f32[256,512]{1,0:T(8,128)S(1)}, u32[]{:S(2)}, u32[]{:S(2)}) collective-permute-start(f32[256,512]{1,0:T(8,128)S(1)} %broadcast_select_fusion.1), channel_id=1, source_target_pairs={{0,4},{4,0},{8,12},{12,8},{1,5},{5,1},{9,13},{13,9},{2,6},{6,2},{1... | collective-permute-start | bytes 1572872 | tf_op jit(solution)/shard_map/ppermute | solution.py:407
  190.3 13.4 %collective-permute-start.6 = (f32[256,512]{1,0:T(8,128)S(1)}, f32[256,512]{1,0:T(8,128)S(1)}, u32[]{:S(2)}, u32[]{:S(2)}) collective-permute-start(f32[256,512]{1,0:T(8,128)S(1)} %broadcast_select_fusion.3), channel_id=1, source_target_pairs={{0,12},{12,0},{4,8},{8,4},{1,13},{13,1},{5,9},{9,5},{2,14},{14,2},... | collective-permute-start | bytes 1572872 | tf_op jit(solution)/shard_map/ppermute | solution.py:405
  193.2 11.9 %collective-permute-start.3 = (f32[512,256]{1,0:T(8,128)S(1)}, f32[512,256]{1,0:T(8,128)S(1)}, u32[]{:S(2)}, u32[]{:S(2)}) collective-permute-start(f32[512,256]{1,0:T(8,128)S(1)} %broadcast_select_fusion.5), channel_id=1, source_target_pairs={{0,1},{1,0},{2,3},{3,2},{4,5},{5,4},{6,7},{7,6},{8,9},{9,8},{10,11... | collective-permute-start | bytes 1572872 | tf_op jit(solution)/shard_map/ppermute | solution.py:406
  194.9 12.8 %collective-permute-start.2 = (f32[512,256]{1,0:T(8,128)S(1)}, f32[512,256]{1,0:T(8,128)S(1)}, u32[]{:S(2)}, u32[]{:S(2)}) collective-permute-start(f32[512,256]{1,0:T(8,128)S(1)} %broadcast_select_fusion.7), channel_id=1, source_target_pairs={{0,3},{3,0},{1,2},{2,1},{4,7},{7,4},{5,6},{6,5},{8,11},{11,8},{9,1... | collective-permute-start | bytes 1572872 | tf_op jit(solution)/shard_map/ppermute | solution.py:404
  209.8 11.9 %collective-permute-start.12 = (f32[256,512]{1,0:T(8,128)S(1)}, f32[256,512]{1,0:T(8,128)S(1)}, u32[]{:S(2)}, u32[]{:S(2)}) collective-permute-start(f32[256,512]{1,0:T(8,128)S(1)} %get-tuple-element.36.refs_6_), channel_id=1, source_target_pairs={{0,4},{4,8},{8,12},{12,0},{1,5},{5,9},{9,13},{13,1},{2,6},{6,10},{... | collective-permute-start | bytes 1572872 | tf_op jit(solution)/shard_map/ppermute | solution.py:400
  210.4 11.2 %collective-permute-start.13 = (f32[256,512]{1,0:T(8,128)S(1)}, f32[256,512]{1,0:T(8,128)S(1)}, u32[]{:S(2)}, u32[]{:S(2)}) collective-permute-start(f32[256,512]{1,0:T(8,128)S(1)} %get-tuple-element.37.refs_9_), channel_id=1, source_target_pairs={{0,12},{4,0},{8,4},{12,8},{1,13},{5,1},{9,5},{13,9},{2,14},{6,2},{... | collective-permute-start | bytes 1572872 | tf_op jit(solution)/shard_map/ppermute | solution.py:401
  213.1 12.1 %collective-permute-start.8 = (f32[512,256]{1,0:T(8,128)S(1)}, f32[512,256]{1,0:T(8,128)S(1)}, u32[]{:S(2)}, u32[]{:S(2)}) collective-permute-start(f32[512,256]{1,0:T(8,128)S(1)} %get-tuple-element.32.refs_0_), channel_id=1, source_target_pairs={{0,1},{1,2},{2,3},{3,0},{4,5},{5,6},{6,7},{7,4},{8,9},{9,10},{10,1... | collective-permute-start | bytes 1572872 | tf_op jit(solution)/shard_map/ppermute | solution.py:398
  213.1 12.1 %collective-permute-start.9 = (f32[512,256]{1,0:T(8,128)S(1)}, f32[512,256]{1,0:T(8,128)S(1)}, u32[]{:S(2)}, u32[]{:S(2)}) collective-permute-start(f32[512,256]{1,0:T(8,128)S(1)} %get-tuple-element.33.refs_3_), channel_id=1, source_target_pairs={{0,3},{1,0},{2,1},{3,2},{4,7},{5,4},{6,5},{7,6},{8,11},{9,8},{10,9... | collective-permute-start | bytes 1572872 | tf_op jit(solution)/shard_map/ppermute | solution.py:399
  221.8 10.0 %collective-permute-start.15 = (f32[256,512]{1,0:T(8,128)S(1)}, f32[256,512]{1,0:T(8,128)S(1)}, u32[]{:S(2)}, u32[]{:S(2)}) collective-permute-start(f32[256,512]{1,0:T(8,128)S(1)} %broadcast_select_fusion), channel_id=1, source_target_pairs={{0,4},{4,0},{8,12},{12,8},{1,5},{5,1},{9,13},{13,9},{2,6},{6,2},{1... | collective-permute-start | bytes 1572872 | tf_op jit(solution)/shard_map/ppermute | solution.py:407
  222.0 11.0 %collective-permute-start.14 = (f32[256,512]{1,0:T(8,128)S(1)}, f32[256,512]{1,0:T(8,128)S(1)}, u32[]{:S(2)}, u32[]{:S(2)}) collective-permute-start(f32[256,512]{1,0:T(8,128)S(1)} %broadcast_select_fusion.2), channel_id=1, source_target_pairs={{0,12},{12,0},{4,8},{8,4},{1,13},{13,1},{5,9},{9,5},{2,14},{14,2},... | collective-permute-start | bytes 1572872 | tf_op jit(solution)/shard_map/ppermute | solution.py:405
  225.3 9.3 %collective-permute-start.11 = (f32[512,256]{1,0:T(8,128)S(1)}, f32[512,256]{1,0:T(8,128)S(1)}, u32[]{:S(2)}, u32[]{:S(2)}) collective-permute-start(f32[512,256]{1,0:T(8,128)S(1)} %broadcast_select_fusion.4), channel_id=1, source_target_pairs={{0,1},{1,0},{2,3},{3,2},{4,5},{5,4},{6,7},{7,6},{8,9},{9,8},{10,11... | collective-permute-start | bytes 1572872 | tf_op jit(solution)/shard_map/ppermute | solution.py:406
  225.5 10.5 %collective-permute-start.10 = (f32[512,256]{1,0:T(8,128)S(1)}, f32[512,256]{1,0:T(8,128)S(1)}, u32[]{:S(2)}, u32[]{:S(2)}) collective-permute-start(f32[512,256]{1,0:T(8,128)S(1)} %broadcast_select_fusion.6), channel_id=1, source_target_pairs={{0,3},{3,0},{1,2},{2,1},{4,7},{7,4},{5,6},{6,5},{8,11},{11,8},{9,1... | collective-permute-start | bytes 1572872 | tf_op jit(solution)/shard_map/ppermute | solution.py:404

commit v3 on v2

--- a/solution.py
+++ b/solution.py
@@ -392,19 +392,41 @@
 CROSS = [(0, 3), (3, 0), (1, 2), (2, 1)]
 
 
+def pick_kernel(axis, near, own, got, out):
+    index = lax.axis_index(axis)
+
+    @pl.when(index == 0)
+    def _():
+        out[...] = own[...]
+
+    @pl.when(index == near)
+    def _():
+        out[...] = got[...]
+
+
+def pick(axis, near, own, got):
+    return pl.pallas_call(
+        lambda *refs: pick_kernel(axis, near, *refs),
+        in_specs=[VMEM] * 2,
+        out_specs=VMEM,
+        out_shape=f32(*own.shape),
+        name="pick",
+        **params(0, 8 * HALF * W),
+    )(own, got)
+
+
 def broadcast(halves, beside=()):
     la, lb, ra, rb = halves
-    row, col = lax.axis_index("row"), lax.axis_index("col")
     la1 = lax.ppermute(la, "col", RIGHT)
     lb1 = lax.ppermute(lb, "col", LEFT)
     ra1 = lax.ppermute(ra, "row", RIGHT)
     rb1 = lax.ppermute(rb, "row", LEFT)
     la1, lb1 = lax.optimization_barrier((la1, lb1))
     ra1, rb1, beside = lax.optimization_barrier((ra1, rb1, beside))
-    la2 = lax.ppermute(jnp.where(col == 1, la1, la), "col", CROSS)
-    ra2 = lax.ppermute(jnp.where(row == 1, ra1, ra), "row", CROSS)
-    lb2 = lax.ppermute(jnp.where(col == 3, lb1, lb), "col", PAIRS)
-    rb2 = lax.ppermute(jnp.where(row == 3, rb1, rb), "row", PAIRS)
+    la2 = lax.ppermute(pick("col", 1, la, la1), "col", CROSS)
+    ra2 = lax.ppermute(pick("row", 1, ra, ra1), "row", CROSS)
+    lb2 = lax.ppermute(pick("col", 3, lb, lb1), "col", PAIRS)
+    rb2 = lax.ppermute(pick("row", 3, rb, rb1), "row", PAIRS)
     return (la, la1, la2, lb, lb1, lb2, ra, ra1, ra2, rb, rb1, rb2), beside
 
 

time: 239 us -> 237 us (level)
  local copies, waits for them, and re-layouts: 5.71 us -> 0.01 us
  waiting for transfers between devices: 24.3 us -> 29.6 us
    ppermute x2, waiting for transfers between devices: 0.01 us -> 10.9 us  [broadcast(): la1 = lax.ppermute(la, 'col', RIGHT)]
    ppermute x2, waiting for transfers between devices: 6.25 us -> 0.01 us  [broadcast(): ra1 = lax.ppermute(ra, 'row', RIGHT)]
    unnamed x12 -> x4, local copies, waits for them, and re-layouts: 5.71 us -> 0.01 us
where the time goes in v3:
time: 237 us
  blocking collectives  161 us (68%)
  waiting for transfers between devices  29.6 us (12%)
  starting transfers between devices  25.1 us (11%)
  Pallas kernels  20.2 us (9%)
    all_to_all x2, blocking collectives, exchange(): return lax.all_to_all(value, PLANE, split_axis=0, concat_axis=0, tiled=True)  161 us
    ppermute x2, waiting for transfers between devices, broadcast(): la1 = lax.ppermute(la, 'col', RIGHT)  10.9 us
    ppermute x2, waiting for transfers between devices, broadcast(): lb2 = lax.ppermute(pick('col', 3, lb, lb1), 'col', PAIRS)  10.2 us
    pallas_call x1, Pallas kernels, permute_tiles(): pl.pallas_call(permute_kernel, in_specs=[HBM] * 4, out_specs=HBM, out_sha...  8.31 us
    ppermute x2, starting transfers between devices, broadcast(): rb1 = lax.ppermute(rb, 'row', LEFT)  6.24 us
    ppermute x2, starting transfers between devices, broadcast(): lb1 = lax.ppermute(lb, 'col', LEFT)  4.89 us
    ppermute x2, starting transfers between devices, broadcast(): la2 = lax.ppermute(pick('col', 1, la, la1), 'col', CROSS)  4.86 us
    ppermute x2, starting transfers between devices, broadcast(): ra2 = lax.ppermute(pick('row', 1, ra, ra1), 'row', CROSS)  4.76 us
  transfers between devices with their start and end apart: 16, of which 10 were waited for; matrix products, arithmetic and copies ran while one was open for 0% of the time, Pallas kernels for 1%

profile of v3, /device:TPU:0, one launch (start us, length us, event | category | flops | bytes accessed | tf_op | source)
XLA Modules:
  0.0 236.5 jit_solution(3333283504457934342)
XLA Ops:
  0.0 8.3 %permute.1 = f32[32,65,8,128]{3,2,1,0:T(8,128)} custom-call(s32[1,32]{1,0:T(1,128)} %bitcast.10, s32[32,256]{1,0:T(8,128)} %rows_hbm.1, s32[32,256]{1,0:T(8,128)} %cols_hbm.1, f32[32,256,256]{2,1,0:T(8,128)} %tiles_hbm.1), custom_call_target="tpu_custom_call" | custom-call | flops 4294967296 | bytes 16777216 | tf_op jit(solution)/shard_map/permute/pallas_call | solution.py:138
  8.3 106.7 %all_to_all.10.strips = f32[32,65,8,128]{3,2,1,0:T(8,128)S(1)} all-to-all(f32[32,65,8,128]{3,2,1,0:T(8,128)} %permute.1), channel_id=1, replica_groups=mesh['front'=8,'row'=4,'col'=4] {'front','row'}, dimensions={0} | all-to-all | bytes 17039360 | tf_op jit(solution)/shard_map/all_to_all | solution.py:386
  115.0 3.6 %reduce.1 = f32[512,2,8,128]{3,2,1,0:T(8,128)S(1)} custom-call(f32[32,65,8,128]{3,2,1,0:T(8,128)S(1)} %all_to_all.10.strips), custom_call_target="tpu_custom_call" | custom-call | flops 2097152 | bytes 12582912 | tf_op jit(solution)/shard_map/reduce/pallas_call | solution.py:176
  118.6 0.0 copy-start
  118.6 0.0 copy-start.1
  118.6 54.7 %all_to_all.11.got = f32[32,16,2,8,128]{4,3,2,1,0:T(8,128)S(1)} all-to-all(f32[32,16,2,8,128]{4,3,2,1,0:T(8,128)S(1)} %bitcast.7), channel_id=1, replica_groups=mesh['front'=8,'row'=4,'col'=4] {'front','row'}, dimensions={0} | all-to-all | bytes 8388608 | tf_op jit(solution)/shard_map/all_to_all | solution.py:386
  173.2 0.0 copy-done
  173.2 0.0 copy-done.1
  173.3 0.7 first_panel.1
  173.9 1.6 collective-permute-start
  175.6 1.7 collective-permute-start.1
  177.2 0.2 collective-permute-start.4
  177.5 3.0 %collective-permute-start.5 = (f32[256,512]{1,0:T(8,128)S(1)}, f32[256,512]{1,0:T(8,128)S(1)}, u32[]{:S(2)}, u32[]{:S(2)}) collective-permute-start(f32[256,512]{1,0:T(8,128)S(1)} %get-tuple-element.28.refs_0_.refs_9_), channel_id=1, source_target_pairs={{0,12},{4,0},{8,4},{12,8},{1,13},{5,1},{9,5},{13,9},{2,14},{6,2},{... | collective-permute-start | bytes 1572872 | tf_op jit(solution)/shard_map/ppermute | solution.py:423
  180.5 0.5 assemble.1.refs_12_
  181.0 7.5 %collective-permute-done.refs_1_ = f32[512,256]{1,0:T(8,128)S(1)} collective-permute-done((f32[512,256]{1,0:T(8,128)S(1)}, f32[512,256]{1,0:T(8,128)S(1)}, u32[]{:S(2)}, u32[]{:S(2)}) %collective-permute-start) | collective-permute-done | bytes 524320 | tf_op jit(solution)/shard_map/ppermute | solution.py:420
  188.5 0.0 collective-permute-done.1.refs_1_.refs_4_
  188.7 1.6 collective-permute-start.3
  190.3 1.7 collective-permute-start.2
  192.0 0.0 collective-permute-done.4.refs_1_.refs_7_
  192.0 0.0 collective-permute-done.5.refs_1_.refs_10_
  192.1 0.1 pick.11
  192.1 0.6 collective-permute-start.7
  192.7 1.7 collective-permute-start.6
  194.5 6.6 %collective-permute-done.3.refs_5_ = f32[512,256]{1,0:T(8,128)S(1)} collective-permute-done((f32[512,256]{1,0:T(8,128)S(1)}, f32[512,256]{1,0:T(8,128)S(1)}, u32[]{:S(2)}, u32[]{:S(2)}) %collective-permute-start.3) | collective-permute-done | bytes 524320 | tf_op jit(solution)/shard_map/ppermute | solution.py:428
  201.1 2.2 collective-permute-done.2.refs_2_
  203.3 0.6 collective-permute-done.7.refs_11_
  203.9 1.8 collective-permute-done.6.refs_8_
  205.7 2.2 second_panel.1
  207.8 0.1 collective-permute-start.8
  207.9 3.2 %collective-permute-start.9 = (f32[512,256]{1,0:T(8,128)S(1)}, f32[512,256]{1,0:T(8,128)S(1)}, u32[]{:S(2)}, u32[]{:S(2)}) collective-permute-start(f32[512,256]{1,0:T(8,128)S(1)} %get-tuple-element.33.refs_0_.refs_3_), channel_id=1, source_target_pairs={{0,3},{1,0},{2,1},{3,2},{4,7},{5,4},{6,5},{7,6},{8,11},{9,8},{10,9... | collective-permute-start | bytes 1572872 | tf_op jit(solution)/shard_map/ppermute | solution.py:421
  211.1 0.0 collective-permute-start.12
  211.1 3.2 %collective-permute-start.13 = (f32[256,512]{1,0:T(8,128)S(1)}, f32[256,512]{1,0:T(8,128)S(1)}, u32[]{:S(2)}, u32[]{:S(2)}) collective-permute-start(f32[256,512]{1,0:T(8,128)S(1)} %get-tuple-element.37.refs_0_.refs_9_), channel_id=1, source_target_pairs={{0,12},{4,0},{8,4},{12,8},{1,13},{5,1},{9,5},{13,9},{2,14},{6,2},{... | collective-permute-start | bytes 1572872 | tf_op jit(solution)/shard_map/ppermute | solution.py:423
  214.4 2.1 update.1.refs_12_
  216.5 3.4 %collective-permute-done.8.refs_1_ = f32[512,256]{1,0:T(8,128)S(1)} collective-permute-done((f32[512,256]{1,0:T(8,128)S(1)}, f32[512,256]{1,0:T(8,128)S(1)}, u32[]{:S(2)}, u32[]{:S(2)}) %collective-permute-start.8) | collective-permute-done | bytes 524320 | tf_op jit(solution)/shard_map/ppermute | solution.py:420
  219.9 0.0 collective-permute-done.9.refs_1_.refs_4_
  220.0 0.1 collective-permute-start.11
  220.1 3.1 %collective-permute-start.10 = (f32[512,256]{1,0:T(8,128)S(1)}, f32[512,256]{1,0:T(8,128)S(1)}, u32[]{:S(2)}, u32[]{:S(2)}) collective-permute-start(f32[512,256]{1,0:T(8,128)S(1)} %pick.12), channel_id=1, source_target_pairs={{0,3},{3,0},{1,2},{2,1},{4,7},{7,4},{5,6},{6,5},{8,11},{11,8},{9,1... | collective-permute-start | bytes 1572872 | tf_op jit(solution)/shard_map/ppermute | solution.py:426
  223.2 0.0 collective-permute-done.12.refs_1_.refs_7_
  223.2 0.0 collective-permute-done.13.refs_1_.refs_10_
  223.3 0.1 pick.15
  223.3 0.1 collective-permute-start.15
  223.4 3.0 %collective-permute-start.14 = (f32[256,512]{1,0:T(8,128)S(1)}, f32[256,512]{1,0:T(8,128)S(1)}, u32[]{:S(2)}, u32[]{:S(2)}) collective-permute-start(f32[256,512]{1,0:T(8,128)S(1)} %pick.14), channel_id=1, source_target_pairs={{0,12},{12,0},{4,8},{8,4},{1,13},{13,1},{5,9},{9,5},{2,14},{14,2},... | collective-permute-start | bytes 1572872 | tf_op jit(solution)/shard_map/ppermute | solution.py:427
  226.5 3.6 %collective-permute-done.11.refs_5_ = f32[512,256]{1,0:T(8,128)S(1)} collective-permute-done((f32[512,256]{1,0:T(8,128)S(1)}, f32[512,256]{1,0:T(8,128)S(1)}, u32[]{:S(2)}, u32[]{:S(2)}) %collective-permute-start.11) | collective-permute-done | bytes 524320 | tf_op jit(solution)/shard_map/ppermute | solution.py:428
  230.0 1.3 collective-permute-done.10.refs_2_
  231.3 1.3 collective-permute-done.15.refs_11_
  232.6 1.3 collective-permute-done.14.refs_8_
  233.9 2.5 %finish.1 = f32[1024,1024]{1,0:T(8,128)} custom-call(f32[512,256]{1,0:T(8,128)S(1)} %get-tuple-element.32.refs_0_, f32[512,256]{1,0:T(8,128)S(1)} %collective-permute-done.8.refs_1_, f32[512,256]{1,0:T(8,128)S(1)} %collective-permute-done.10.refs_2_, f32[512,256]{1,0:T(8,128)S(1)} %get-tuple-element.33.refs_0_.refs_3_, ...), custom_call_target="tpu_custom_call" | custom-call | flops 1610612736 | bytes 10485760 | tf_op jit(solution)/shard_map/finish/pallas_call | solution.py:374
  (6 shorter events, 0.2 us)
Async XLA Ops:
  118.6 54.7 %copy-start = (f32[1,1024,1024]{2,1,0:T(8,128)S(1)}, f32[1,1024,1024]{2,1,0:T(8,128)}, u32[]{:S(2)}) copy-start(f32[1,1024,1024]{2,1,0:T(8,128)} %param.6) | copy-start | bytes 12582916
  118.6 54.7 %copy-start.1 = (f32[1,2,256,256]{3,2,1,0:T(8,128)S(1)}, f32[1,2,256,256]{3,2,1,0:T(8,128)}, u32[]{:S(2)}) copy-start(f32[1,2,256,256]{3,2,1,0:T(8,128)} %param.11) | copy-start | bytes 1572868
  173.9 14.6 %collective-permute-start = (f32[512,256]{1,0:T(8,128)S(1)}, f32[512,256]{1,0:T(8,128)S(1)}, u32[]{:S(2)}, u32[]{:S(2)}) collective-permute-start(f32[512,256]{1,0:T(8,128)S(1)} %get-tuple-element.23.refs_0_), channel_id=1, source_target_pairs={{0,1},{1,2},{2,3},{3,0},{4,5},{5,6},{6,7},{7,4},{8,9},{9,10},{10,1... | collective-permute-start | bytes 1572872 | tf_op jit(solution)/shard_map/ppermute | solution.py:420
  175.6 13.0 %collective-permute-start.1 = (f32[512,256]{1,0:T(8,128)S(1)}, f32[512,256]{1,0:T(8,128)S(1)}, u32[]{:S(2)}, u32[]{:S(2)}) collective-permute-start(f32[512,256]{1,0:T(8,128)S(1)} %get-tuple-element.24.refs_0_.refs_3_), channel_id=1, source_target_pairs={{0,3},{1,0},{2,1},{3,2},{4,7},{5,4},{6,5},{7,6},{8,11},{9,8},{10,9... | collective-permute-start | bytes 1572872 | tf_op jit(solution)/shard_map/ppermute | solution.py:421
  177.2 14.8 %collective-permute-start.4 = (f32[256,512]{1,0:T(8,128)S(1)}, f32[256,512]{1,0:T(8,128)S(1)}, u32[]{:S(2)}, u32[]{:S(2)}) collective-permute-start(f32[256,512]{1,0:T(8,128)S(1)} %get-tuple-element.27.refs_0_.refs_6_), channel_id=1, source_target_pairs={{0,4},{4,8},{8,12},{12,0},{1,5},{5,9},{9,13},{13,1},{2,6},{6,10},{... | collective-permute-start | bytes 1572872 | tf_op jit(solution)/shard_map/ppermute | solution.py:422
  177.5 14.6 %collective-permute-start.5 = (f32[256,512]{1,0:T(8,128)S(1)}, f32[256,512]{1,0:T(8,128)S(1)}, u32[]{:S(2)}, u32[]{:S(2)}) collective-permute-start(f32[256,512]{1,0:T(8,128)S(1)} %get-tuple-element.28.refs_0_.refs_9_), channel_id=1, source_target_pairs={{0,12},{4,0},{8,4},{12,8},{1,13},{5,1},{9,5},{13,9},{2,14},{6,2},{... | collective-permute-start | bytes 1572872 | tf_op jit(solution)/shard_map/ppermute | solution.py:423
  188.7 12.5 %collective-permute-start.3 = (f32[512,256]{1,0:T(8,128)S(1)}, f32[512,256]{1,0:T(8,128)S(1)}, u32[]{:S(2)}, u32[]{:S(2)}) collective-permute-start(f32[512,256]{1,0:T(8,128)S(1)} %pick.9), channel_id=1, source_target_pairs={{0,1},{1,0},{2,3},{3,2},{4,5},{5,4},{6,7},{7,6},{8,9},{9,8},{10,11... | collective-permute-start | bytes 1572872 | tf_op jit(solution)/shard_map/ppermute | solution.py:428
  190.3 13.0 %collective-permute-start.2 = (f32[512,256]{1,0:T(8,128)S(1)}, f32[512,256]{1,0:T(8,128)S(1)}, u32[]{:S(2)}, u32[]{:S(2)}) collective-permute-start(f32[512,256]{1,0:T(8,128)S(1)} %pick.8), channel_id=1, source_target_pairs={{0,3},{3,0},{1,2},{2,1},{4,7},{7,4},{5,6},{6,5},{8,11},{11,8},{9,1... | collective-permute-start | bytes 1572872 | tf_op jit(solution)/shard_map/ppermute | solution.py:426
  192.1 11.7 %collective-permute-start.7 = (f32[256,512]{1,0:T(8,128)S(1)}, f32[256,512]{1,0:T(8,128)S(1)}, u32[]{:S(2)}, u32[]{:S(2)}) collective-permute-start(f32[256,512]{1,0:T(8,128)S(1)} %pick.11), channel_id=1, source_target_pairs={{0,4},{4,0},{8,12},{12,8},{1,5},{5,1},{9,13},{13,9},{2,6},{6,2},{1... | collective-permute-start | bytes 1572872 | tf_op jit(solution)/shard_map/ppermute | solution.py:429
  192.7 12.9 %collective-permute-start.6 = (f32[256,512]{1,0:T(8,128)S(1)}, f32[256,512]{1,0:T(8,128)S(1)}, u32[]{:S(2)}, u32[]{:S(2)}) collective-permute-start(f32[256,512]{1,0:T(8,128)S(1)} %pick.10), channel_id=1, source_target_pairs={{0,12},{12,0},{4,8},{8,4},{1,13},{13,1},{5,9},{9,5},{2,14},{14,2},... | collective-permute-start | bytes 1572872 | tf_op jit(solution)/shard_map/ppermute | solution.py:427
  207.8 12.1 %collective-permute-start.8 = (f32[512,256]{1,0:T(8,128)S(1)}, f32[512,256]{1,0:T(8,128)S(1)}, u32[]{:S(2)}, u32[]{:S(2)}) collective-permute-start(f32[512,256]{1,0:T(8,128)S(1)} %get-tuple-element.32.refs_0_), channel_id=1, source_target_pairs={{0,1},{1,2},{2,3},{3,0},{4,5},{5,6},{6,7},{7,4},{8,9},{9,10},{10,1... | collective-permute-start | bytes 1572872 | tf_op jit(solution)/shard_map/ppermute | solution.py:420
  207.9 12.0 %collective-permute-start.9 = (f32[512,256]{1,0:T(8,128)S(1)}, f32[512,256]{1,0:T(8,128)S(1)}, u32[]{:S(2)}, u32[]{:S(2)}) collective-permute-start(f32[512,256]{1,0:T(8,128)S(1)} %get-tuple-element.33.refs_0_.refs_3_), channel_id=1, source_target_pairs={{0,3},{1,0},{2,1},{3,2},{4,7},{5,4},{6,5},{7,6},{8,11},{9,8},{10,9... | collective-permute-start | bytes 1572872 | tf_op jit(solution)/shard_map/ppermute | solution.py:421
  211.1 12.1 %collective-permute-start.12 = (f32[256,512]{1,0:T(8,128)S(1)}, f32[256,512]{1,0:T(8,128)S(1)}, u32[]{:S(2)}, u32[]{:S(2)}) collective-permute-start(f32[256,512]{1,0:T(8,128)S(1)} %get-tuple-element.36.refs_0_.refs_6_), channel_id=1, source_target_pairs={{0,4},{4,8},{8,12},{12,0},{1,5},{5,9},{9,13},{13,1},{2,6},{6,10},{... | collective-permute-start | bytes 1572872 | tf_op jit(solution)/shard_map/ppermute | solution.py:422
  211.1 12.1 %collective-permute-start.13 = (f32[256,512]{1,0:T(8,128)S(1)}, f32[256,512]{1,0:T(8,128)S(1)}, u32[]{:S(2)}, u32[]{:S(2)}) collective-permute-start(f32[256,512]{1,0:T(8,128)S(1)} %get-tuple-element.37.refs_0_.refs_9_), channel_id=1, source_target_pairs={{0,12},{4,0},{8,4},{12,8},{1,13},{5,1},{9,5},{13,9},{2,14},{6,2},{... | collective-permute-start | bytes 1572872 | tf_op jit(solution)/shard_map/ppermute | solution.py:423
  220.0 10.0 %collective-permute-start.11 = (f32[512,256]{1,0:T(8,128)S(1)}, f32[512,256]{1,0:T(8,128)S(1)}, u32[]{:S(2)}, u32[]{:S(2)}) collective-permute-start(f32[512,256]{1,0:T(8,128)S(1)} %pick.13), channel_id=1, source_target_pairs={{0,1},{1,0},{2,3},{3,2},{4,5},{5,4},{6,7},{7,6},{8,9},{9,8},{10,11... | collective-permute-start | bytes 1572872 | tf_op jit(solution)/shard_map/ppermute | solution.py:428
  220.1 11.2 %collective-permute-start.10 = (f32[512,256]{1,0:T(8,128)S(1)}, f32[512,256]{1,0:T(8,128)S(1)}, u32[]{:S(2)}, u32[]{:S(2)}) collective-permute-start(f32[512,256]{1,0:T(8,128)S(1)} %pick.12), channel_id=1, source_target_pairs={{0,3},{3,0},{1,2},{2,1},{4,7},{7,4},{5,6},{6,5},{8,11},{11,8},{9,1... | collective-permute-start | bytes 1572872 | tf_op jit(solution)/shard_map/ppermute | solution.py:426
  223.3 9.3 %collective-permute-start.15 = (f32[256,512]{1,0:T(8,128)S(1)}, f32[256,512]{1,0:T(8,128)S(1)}, u32[]{:S(2)}, u32[]{:S(2)}) collective-permute-start(f32[256,512]{1,0:T(8,128)S(1)} %pick.15), channel_id=1, source_target_pairs={{0,4},{4,0},{8,12},{12,8},{1,5},{5,1},{9,13},{13,9},{2,6},{6,2},{1... | collective-permute-start | bytes 1572872 | tf_op jit(solution)/shard_map/ppermute | solution.py:429
  223.4 10.5 %collective-permute-start.14 = (f32[256,512]{1,0:T(8,128)S(1)}, f32[256,512]{1,0:T(8,128)S(1)}, u32[]{:S(2)}, u32[]{:S(2)}) collective-permute-start(f32[256,512]{1,0:T(8,128)S(1)} %pick.14), channel_id=1, source_target_pairs={{0,12},{12,0},{4,8},{8,4},{1,13},{13,1},{5,9},{9,5},{2,14},{14,2},... | collective-permute-start | bytes 1572872 | tf_op jit(solution)/shard_map/ppermute | solution.py:427

commit v4 on v3

--- a/solution.py
+++ b/solution.py
@@ -386,8 +386,6 @@
     return lax.all_to_all(value, PLANE, split_axis=0, concat_axis=0, tiled=True)
 
 
-RIGHT = [(k, (k + 1) % RING) for k in range(RING)]
-LEFT = [(k, (k - 1) % RING) for k in range(RING)]
 PAIRS = [(0, 1), (1, 0), (2, 3), (3, 2)]
 CROSS = [(0, 3), (3, 0), (1, 2), (2, 1)]
 
@@ -417,10 +415,10 @@
 
 def broadcast(halves, beside=()):
     la, lb, ra, rb = halves
-    la1 = lax.ppermute(la, "col", RIGHT)
-    lb1 = lax.ppermute(lb, "col", LEFT)
-    ra1 = lax.ppermute(ra, "row", RIGHT)
-    rb1 = lax.ppermute(rb, "row", LEFT)
+    la1 = lax.ppermute(la, "col", PAIRS)
+    lb1 = lax.ppermute(lb, "col", CROSS)
+    ra1 = lax.ppermute(ra, "row", PAIRS)
+    rb1 = lax.ppermute(rb, "row", CROSS)
     la1, lb1 = lax.optimization_barrier((la1, lb1))
     ra1, rb1, beside = lax.optimization_barrier((ra1, rb1, beside))
     la2 = lax.ppermute(pick("col", 1, la, la1), "col", CROSS)

time: 237 us -> 236 us (level)
  starting transfers between devices: 25.1 us -> 15.4 us
  waiting for transfers between devices: 29.6 us -> 38 us
    ppermute x8, waiting for transfers between devices: 10.9 us -> 17.3 us  [the longest x2 13.5 us: broadcast(): la1 = lax.ppermute(la, 'col', PAIRS)]
    ppermute x8, starting transfers between devices: 13.1 us -> 8.14 us  [the longest x2 3.12 us: broadcast(): lb1 = lax.ppermute(lb, 'col', CROSS)]
    ppermute x2, waiting for transfers between devices: 10.2 us -> 14.7 us  [broadcast(): lb2 = lax.ppermute(pick('col', 3, lb, lb1), 'col', PAIRS)]
  transfers between devices with their start and end apart: 16 -> 16, of which waited for: 10 -> 11; matrix products, arithmetic and copies ran while one was open for 0% -> 0% of each run, Pallas kernels for 1% -> 1%
where the time goes in v4:
time: 236 us; the launch traced here: 235 us
  blocking collectives  161 us (68%)
  waiting for transfers between devices  38 us (16%)
  Pallas kernels  20.1 us (9%)
  starting transfers between devices  15.4 us (7%)
    all_to_all x2, blocking collectives, exchange(): return lax.all_to_all(value, PLANE, split_axis=0, concat_axis=0, tiled=True)  161 us
    ppermute x2, waiting for transfers between devices, broadcast(): lb2 = lax.ppermute(pick('col', 3, lb, lb1), 'col', PAIRS)  14.7 us
    ppermute x2, waiting for transfers between devices, broadcast(): la1 = lax.ppermute(la, 'col', PAIRS)  13.5 us
    pallas_call x1, Pallas kernels, permute_tiles(): pl.pallas_call(permute_kernel, in_specs=[HBM] * 4, out_specs=HBM, out_sha...  8.31 us
  transfers between devices with their start and end apart: 16, of which 11 were waited for; matrix products, arithmetic and copies ran while one was open for 0% of the time, Pallas kernels for 1%

profile of v4, /device:TPU:0, one launch (start us, length us, event | category | flops | bytes accessed | tf_op | source)
XLA Modules:
  0.0 235.2 jit_solution(6142179917490024096)
XLA Ops:
  0.0 8.3 %permute.1 = f32[32,65,8,128]{3,2,1,0:T(8,128)} custom-call(s32[1,32]{1,0:T(1,128)} %bitcast.10, s32[32,256]{1,0:T(8,128)} %rows_hbm.1, s32[32,256]{1,0:T(8,128)} %cols_hbm.1, f32[32,256,256]{2,1,0:T(8,128)} %tiles_hbm.1), custom_call_target="tpu_custom_call" | custom-call | flops 4294967296 | bytes 16777216 | tf_op jit(solution)/shard_map/permute/pallas_call | solution.py:138
  8.3 106.7 %all_to_all.10.strips = f32[32,65,8,128]{3,2,1,0:T(8,128)S(1)} all-to-all(f32[32,65,8,128]{3,2,1,0:T(8,128)} %permute.1), channel_id=1, replica_groups=mesh['front'=8,'row'=4,'col'=4] {'front','row'}, dimensions={0} | all-to-all | bytes 17039360 | tf_op jit(solution)/shard_map/all_to_all | solution.py:386
  115.0 3.6 %reduce.1 = f32[512,2,8,128]{3,2,1,0:T(8,128)S(1)} custom-call(f32[32,65,8,128]{3,2,1,0:T(8,128)S(1)} %all_to_all.10.strips), custom_call_target="tpu_custom_call" | custom-call | flops 2097152 | bytes 12582912 | tf_op jit(solution)/shard_map/reduce/pallas_call | solution.py:176
  118.6 0.0 copy-start
  118.6 0.0 copy-start.1
  118.6 54.7 %all_to_all.11.got = f32[32,16,2,8,128]{4,3,2,1,0:T(8,128)S(1)} all-to-all(f32[32,16,2,8,128]{4,3,2,1,0:T(8,128)S(1)} %bitcast.7), channel_id=1, replica_groups=mesh['front'=8,'row'=4,'col'=4] {'front','row'}, dimensions={0} | all-to-all | bytes 8388608 | tf_op jit(solution)/shard_map/all_to_all | solution.py:386
  173.2 0.0 copy-done
  173.2 0.0 copy-done.1
  173.3 0.7 first_panel.1
  173.9 1.7 collective-permute-start
  175.6 2.2 collective-permute-start.1
  177.8 0.2 collective-permute-start.4
  178.0 2.1 collective-permute-start.5
  180.1 0.5 assemble.1.refs_12_
  180.6 6.6 %collective-permute-done.refs_1_ = f32[512,256]{1,0:T(8,128)S(1)} collective-permute-done((f32[512,256]{1,0:T(8,128)S(1)}, f32[512,256]{1,0:T(8,128)S(1)}, u32[]{:S(2)}, u32[]{:S(2)}) %collective-permute-start) | collective-permute-done | bytes 524320 | tf_op jit(solution)/shard_map/ppermute | solution.py:418
  187.3 2.5 %collective-permute-done.1.refs_1_.refs_4_ = f32[512,256]{1,0:T(8,128)S(1)} collective-permute-done((f32[512,256]{1,0:T(8,128)S(1)}, f32[512,256]{1,0:T(8,128)S(1)}, u32[]{:S(2)}, u32[]{:S(2)}) %collective-permute-start.1) | collective-permute-done | bytes 524320 | tf_op jit(solution)/shard_map/ppermute | solution.py:419
  189.9 0.1 collective-permute-start.3
  190.0 2.2 collective-permute-start.2
  192.2 0.0 collective-permute-done.4.refs_1_.refs_7_
  192.2 0.0 collective-permute-done.5.refs_1_.refs_10_
  192.2 0.1 pick.11
  192.3 0.6 collective-permute-start.7
  192.9 1.7 collective-permute-start.6
  194.6 7.4 %collective-permute-done.3.refs_5_ = f32[512,256]{1,0:T(8,128)S(1)} collective-permute-done((f32[512,256]{1,0:T(8,128)S(1)}, f32[512,256]{1,0:T(8,128)S(1)}, u32[]{:S(2)}, u32[]{:S(2)}) %collective-permute-start.3) | collective-permute-done | bytes 524320 | tf_op jit(solution)/shard_map/ppermute | solution.py:426
  202.0 1.3 collective-permute-done.2.refs_2_
  203.3 0.8 collective-permute-done.7.refs_11_
  204.1 1.8 collective-permute-done.6.refs_8_
  205.9 2.1 second_panel.1
  208.0 0.1 collective-permute-start.8
  208.1 0.9 collective-permute-start.9
  209.1 0.0 collective-permute-start.12
  209.1 1.0 collective-permute-start.13
  210.1 2.1 update.1.refs_12_
  212.2 6.8 %collective-permute-done.8.refs_1_ = f32[512,256]{1,0:T(8,128)S(1)} collective-permute-done((f32[512,256]{1,0:T(8,128)S(1)}, f32[512,256]{1,0:T(8,128)S(1)}, u32[]{:S(2)}, u32[]{:S(2)}) %collective-permute-start.8) | collective-permute-done | bytes 524320 | tf_op jit(solution)/shard_map/ppermute | solution.py:418
  219.0 1.3 collective-permute-done.9.refs_1_.refs_4_
  220.4 0.5 collective-permute-start.11
  220.9 0.7 collective-permute-start.10
  221.7 0.0 collective-permute-done.12.refs_1_.refs_7_
  221.7 0.0 collective-permute-done.13.refs_1_.refs_10_
  221.7 0.1 pick.15
  221.8 0.1 collective-permute-start.15
  221.9 1.3 collective-permute-start.14
  223.1 7.3 %collective-permute-done.11.refs_5_ = f32[512,256]{1,0:T(8,128)S(1)} collective-permute-done((f32[512,256]{1,0:T(8,128)S(1)}, f32[512,256]{1,0:T(8,128)S(1)}, u32[]{:S(2)}, u32[]{:S(2)}) %collective-permute-start.11) | collective-permute-done | bytes 524320 | tf_op jit(solution)/shard_map/ppermute | solution.py:426
  230.5 1.3 collective-permute-done.10.refs_2_
  231.8 0.0 collective-permute-done.15.refs_11_
  231.8 0.8 collective-permute-done.14.refs_8_
  232.5 2.5 %finish.1 = f32[1024,1024]{1,0:T(8,128)} custom-call(f32[512,256]{1,0:T(8,128)S(1)} %get-tuple-element.32.refs_0_, f32[512,256]{1,0:T(8,128)S(1)} %collective-permute-done.8.refs_1_, f32[512,256]{1,0:T(8,128)S(1)} %collective-permute-done.10.refs_2_, f32[512,256]{1,0:T(8,128)S(1)} %get-tuple-element.33.refs_0_.refs_3_, ...), custom_call_target="tpu_custom_call" | custom-call | flops 1610612736 | bytes 10485760 | tf_op jit(solution)/shard_map/finish/pallas_call | solution.py:374
  (6 shorter events, 0.2 us)
Async XLA Ops:
  118.6 54.7 %copy-start = (f32[1,1024,1024]{2,1,0:T(8,128)S(1)}, f32[1,1024,1024]{2,1,0:T(8,128)}, u32[]{:S(2)}) copy-start(f32[1,1024,1024]{2,1,0:T(8,128)} %param.6) | copy-start | bytes 12582916
  118.6 54.7 %copy-start.1 = (f32[1,2,256,256]{3,2,1,0:T(8,128)S(1)}, f32[1,2,256,256]{3,2,1,0:T(8,128)}, u32[]{:S(2)}) copy-start(f32[1,2,256,256]{3,2,1,0:T(8,128)} %param.11) | copy-start | bytes 1572868
  173.9 13.3 %collective-permute-start = (f32[512,256]{1,0:T(8,128)S(1)}, f32[512,256]{1,0:T(8,128)S(1)}, u32[]{:S(2)}, u32[]{:S(2)}) collective-permute-start(f32[512,256]{1,0:T(8,128)S(1)} %get-tuple-element.23.refs_0_), channel_id=1, source_target_pairs={{0,1},{1,0},{2,3},{3,2},{4,5},{5,4},{6,7},{7,6},{8,9},{9,8},{10,11... | collective-permute-start | bytes 1572872 | tf_op jit(solution)/shard_map/ppermute | solution.py:418
  175.6 14.2 %collective-permute-start.1 = (f32[512,256]{1,0:T(8,128)S(1)}, f32[512,256]{1,0:T(8,128)S(1)}, u32[]{:S(2)}, u32[]{:S(2)}) collective-permute-start(f32[512,256]{1,0:T(8,128)S(1)} %get-tuple-element.24.refs_0_.refs_3_), channel_id=1, source_target_pairs={{0,3},{3,0},{1,2},{2,1},{4,7},{7,4},{5,6},{6,5},{8,11},{11,8},{9,1... | collective-permute-start | bytes 1572872 | tf_op jit(solution)/shard_map/ppermute | solution.py:419
  177.8 14.4 %collective-permute-start.4 = (f32[256,512]{1,0:T(8,128)S(1)}, f32[256,512]{1,0:T(8,128)S(1)}, u32[]{:S(2)}, u32[]{:S(2)}) collective-permute-start(f32[256,512]{1,0:T(8,128)S(1)} %get-tuple-element.27.refs_0_.refs_6_), channel_id=1, source_target_pairs={{0,4},{4,0},{8,12},{12,8},{1,5},{5,1},{9,13},{13,9},{2,6},{6,2},{1... | collective-permute-start | bytes 1572872 | tf_op jit(solution)/shard_map/ppermute | solution.py:420
  178.0 14.2 %collective-permute-start.5 = (f32[256,512]{1,0:T(8,128)S(1)}, f32[256,512]{1,0:T(8,128)S(1)}, u32[]{:S(2)}, u32[]{:S(2)}) collective-permute-start(f32[256,512]{1,0:T(8,128)S(1)} %get-tuple-element.28.refs_0_.refs_9_), channel_id=1, source_target_pairs={{0,12},{12,0},{4,8},{8,4},{1,13},{13,1},{5,9},{9,5},{2,14},{14,2},... | collective-permute-start | bytes 1572872 | tf_op jit(solution)/shard_map/ppermute | solution.py:421
  189.9 12.1 %collective-permute-start.3 = (f32[512,256]{1,0:T(8,128)S(1)}, f32[512,256]{1,0:T(8,128)S(1)}, u32[]{:S(2)}, u32[]{:S(2)}) collective-permute-start(f32[512,256]{1,0:T(8,128)S(1)} %pick.9), channel_id=1, source_target_pairs={{0,1},{1,0},{2,3},{3,2},{4,5},{5,4},{6,7},{7,6},{8,9},{9,8},{10,11... | collective-permute-start | bytes 1572872 | tf_op jit(solution)/shard_map/ppermute | solution.py:426
  190.0 13.3 %collective-permute-start.2 = (f32[512,256]{1,0:T(8,128)S(1)}, f32[512,256]{1,0:T(8,128)S(1)}, u32[]{:S(2)}, u32[]{:S(2)}) collective-permute-start(f32[512,256]{1,0:T(8,128)S(1)} %pick.8), channel_id=1, source_target_pairs={{0,3},{3,0},{1,2},{2,1},{4,7},{7,4},{5,6},{6,5},{8,11},{11,8},{9,1... | collective-permute-start | bytes 1572872 | tf_op jit(solution)/shard_map/ppermute | solution.py:424
  192.3 11.9 %collective-permute-start.7 = (f32[256,512]{1,0:T(8,128)S(1)}, f32[256,512]{1,0:T(8,128)S(1)}, u32[]{:S(2)}, u32[]{:S(2)}) collective-permute-start(f32[256,512]{1,0:T(8,128)S(1)} %pick.11), channel_id=1, source_target_pairs={{0,4},{4,0},{8,12},{12,8},{1,5},{5,1},{9,13},{13,9},{2,6},{6,2},{1... | collective-permute-start | bytes 1572872 | tf_op jit(solution)/shard_map/ppermute | solution.py:427
  192.9 13.0 %collective-permute-start.6 = (f32[256,512]{1,0:T(8,128)S(1)}, f32[256,512]{1,0:T(8,128)S(1)}, u32[]{:S(2)}, u32[]{:S(2)}) collective-permute-start(f32[256,512]{1,0:T(8,128)S(1)} %pick.10), channel_id=1, source_target_pairs={{0,12},{12,0},{4,8},{8,4},{1,13},{13,1},{5,9},{9,5},{2,14},{14,2},... | collective-permute-start | bytes 1572872 | tf_op jit(solution)/shard_map/ppermute | solution.py:425
  208.0 11.0 %collective-permute-start.8 = (f32[512,256]{1,0:T(8,128)S(1)}, f32[512,256]{1,0:T(8,128)S(1)}, u32[]{:S(2)}, u32[]{:S(2)}) collective-permute-start(f32[512,256]{1,0:T(8,128)S(1)} %get-tuple-element.32.refs_0_), channel_id=1, source_target_pairs={{0,1},{1,0},{2,3},{3,2},{4,5},{5,4},{6,7},{7,6},{8,9},{9,8},{10,11... | collective-permute-start | bytes 1572872 | tf_op jit(solution)/shard_map/ppermute | solution.py:418
  208.1 12.2 %collective-permute-start.9 = (f32[512,256]{1,0:T(8,128)S(1)}, f32[512,256]{1,0:T(8,128)S(1)}, u32[]{:S(2)}, u32[]{:S(2)}) collective-permute-start(f32[512,256]{1,0:T(8,128)S(1)} %get-tuple-element.33.refs_0_.refs_3_), channel_id=1, source_target_pairs={{0,3},{3,0},{1,2},{2,1},{4,7},{7,4},{5,6},{6,5},{8,11},{11,8},{9,1... | collective-permute-start | bytes 1572872 | tf_op jit(solution)/shard_map/ppermute | solution.py:419
  209.1 12.6 %collective-permute-start.12 = (f32[256,512]{1,0:T(8,128)S(1)}, f32[256,512]{1,0:T(8,128)S(1)}, u32[]{:S(2)}, u32[]{:S(2)}) collective-permute-start(f32[256,512]{1,0:T(8,128)S(1)} %get-tuple-element.36.refs_0_.refs_6_), channel_id=1, source_target_pairs={{0,4},{4,0},{8,12},{12,8},{1,5},{5,1},{9,13},{13,9},{2,6},{6,2},{1... | collective-permute-start | bytes 1572872 | tf_op jit(solution)/shard_map/ppermute | solution.py:420
  209.1 12.6 %collective-permute-start.13 = (f32[256,512]{1,0:T(8,128)S(1)}, f32[256,512]{1,0:T(8,128)S(1)}, u32[]{:S(2)}, u32[]{:S(2)}) collective-permute-start(f32[256,512]{1,0:T(8,128)S(1)} %get-tuple-element.37.refs_0_.refs_9_), channel_id=1, source_target_pairs={{0,12},{12,0},{4,8},{8,4},{1,13},{13,1},{5,9},{9,5},{2,14},{14,2},... | collective-permute-start | bytes 1572872 | tf_op jit(solution)/shard_map/ppermute | solution.py:421
  220.4 10.0 %collective-permute-start.11 = (f32[512,256]{1,0:T(8,128)S(1)}, f32[512,256]{1,0:T(8,128)S(1)}, u32[]{:S(2)}, u32[]{:S(2)}) collective-permute-start(f32[512,256]{1,0:T(8,128)S(1)} %pick.13), channel_id=1, source_target_pairs={{0,1},{1,0},{2,3},{3,2},{4,5},{5,4},{6,7},{7,6},{8,9},{9,8},{10,11... | collective-permute-start | bytes 1572872 | tf_op jit(solution)/shard_map/ppermute | solution.py:426
  220.9 10.9 %collective-permute-start.10 = (f32[512,256]{1,0:T(8,128)S(1)}, f32[512,256]{1,0:T(8,128)S(1)}, u32[]{:S(2)}, u32[]{:S(2)}) collective-permute-start(f32[512,256]{1,0:T(8,128)S(1)} %pick.12), channel_id=1, source_target_pairs={{0,3},{3,0},{1,2},{2,1},{4,7},{7,4},{5,6},{6,5},{8,11},{11,8},{9,1... | collective-permute-start | bytes 1572872 | tf_op jit(solution)/shard_map/ppermute | solution.py:424
  221.8 10.0 %collective-permute-start.15 = (f32[256,512]{1,0:T(8,128)S(1)}, f32[256,512]{1,0:T(8,128)S(1)}, u32[]{:S(2)}, u32[]{:S(2)}) collective-permute-start(f32[256,512]{1,0:T(8,128)S(1)} %pick.15), channel_id=1, source_target_pairs={{0,4},{4,0},{8,12},{12,8},{1,5},{5,1},{9,13},{13,9},{2,6},{6,2},{1... | collective-permute-start | bytes 1572872 | tf_op jit(solution)/shard_map/ppermute | solution.py:427
  221.9 10.7 %collective-permute-start.14 = (f32[256,512]{1,0:T(8,128)S(1)}, f32[256,512]{1,0:T(8,128)S(1)}, u32[]{:S(2)}, u32[]{:S(2)}) collective-permute-start(f32[256,512]{1,0:T(8,128)S(1)} %pick.14), channel_id=1, source_target_pairs={{0,12},{12,0},{4,8},{8,4},{1,13},{13,1},{5,9},{9,5},{2,14},{14,2},... | collective-permute-start | bytes 1572872 | tf_op jit(solution)/shard_map/ppermute | solution.py:425

commit v5 on v4

--- a/solution.py
+++ b/solution.py
@@ -13,7 +13,7 @@
 STRIP = 8
 LANES = 128
 NJ = 32
-RING = 4
+ANY = pl.BlockSpec(memory_space=pl.ANY)
 HBM = pl.BlockSpec(memory_space=pltpu.HBM)
 VMEM = pl.BlockSpec(memory_space=pltpu.VMEM)
 DMA = pltpu.SemaphoreType.DMA
@@ -196,26 +196,38 @@
     return jnp.concatenate([left, right], axis=1)
 
 
-def first_kernel(parent, got, inv_ref, la, lb, ra, rb):
+def first_factor_kernel(parent, got, inv_ref, la, lb):
     inv = split(inv_ref[0])
     for k in range(SUBS):
         half = slice(k % 2 * W, (k % 2 + 1) * W)
         (la, lb)[k // 2][half] = dot3(split(block(parent, got, k, 0)), inv)
-        (ra, rb)[k // 2][:, half] = block(parent, got, 0, k)
-
-
-HALVES = [f32(HALF, W), f32(HALF, W), f32(W, HALF), f32(W, HALF)]
-
-
-def first_panel(parent, got, inverses):
-    return pl.pallas_call(
-        first_kernel,
+
+
+def first_factor(parent, got, inverses):
+    return pl.pallas_call(
+        first_factor_kernel,
         in_specs=[VMEM] * 3,
-        out_specs=[VMEM] * 4,
-        out_shape=HALVES,
-        name="first_panel",
+        out_specs=[VMEM] * 2,
+        out_shape=[f32(HALF, W)] * 2,
+        name="first_factor",
         **params(6 * FULL * W * W, 12 * FULL * W),
     )(parent, got, inverses)
+
+
+def first_rows_kernel(parent, got, after, ra, rb):
+    for k in range(SUBS):
+        (ra, rb)[k // 2][:, k % 2 * W : (k % 2 + 1) * W] = block(parent, got, 0, k)
+
+
+def first_rows(parent, got, after):
+    return pl.pallas_call(
+        first_rows_kernel,
+        in_specs=[VMEM] * 2 + [ANY],
+        out_specs=[VMEM] * 2,
+        out_shape=[f32(W, HALF)] * 2,
+        name="first_rows",
+        **params(FULL * W, 12 * FULL * W),
+    )(parent, got, after)
 
 
 def assemble_kernel(parent, got, matrix):
@@ -259,44 +271,59 @@
     choose(row, 3, pieces[9:12], right.at[:, pl.ds(HALF, HALF)])
 
 
-def second_kernel(*refs):
-    pieces = refs[:12]
-    matrix, inv_ref, la, lb, ra, rb, left, right = refs[12:]
-    row, col = lax.axis_index("row"), lax.axis_index("col")
-
-    @pl.when((row == 0) | (col == 0))
-    def _():
-        choose_all(row, col, pieces, left, right)
-
-    @pl.when(col == 0)
-    def _():
+def second_factor_kernel(*refs):
+    pieces = refs[:9]
+    matrix, inv_ref, la, lb, right = refs[9:]
+
+    @pl.when(lax.axis_index("col") == 0)
+    def _():
+        choose(lax.axis_index("row"), 1, pieces[6:9], right)
         inv = split(inv_ref[1])
-        corner = split(right[:, W:HALF])
+        corner = split(right[:, W:])
         for k in range(SUBS):
             at = slice(k * W, (k + 1) * W)
             half = slice(k % 2 * W, (k % 2 + 1) * W)
-            reduced = matrix[at, W:HALF] - dot3(split(left[at]), corner)
+            reduced = matrix[at, W:HALF] - dot3(split(pieces[3 * (k // 2)][half]), corner)
             (la, lb)[k // 2][half] = dot3(split(reduced), inv)
 
-    @pl.when(row == 0)
-    def _():
-        below = split(left[W:HALF])
+
+def second_factor(pieces, matrix, inverses):
+    return pl.pallas_call(
+        second_factor_kernel,
+        in_specs=[VMEM] * 11,
+        out_specs=[VMEM] * 2,
+        out_shape=[f32(HALF, W)] * 2,
+        scratch_shapes=[space(W, HALF)],
+        name="second_factor",
+        **params(12 * FULL * W * W, 16 * FULL * W),
+    )(*pieces[:9], matrix, inverses)
+
+
+def second_rows_kernel(*refs):
+    pieces = refs[:9]
+    matrix, after, ra, rb, left = refs[9:]
+
+    @pl.when(lax.axis_index("row") == 0)
+    def _():
+        choose(lax.axis_index("col"), 1, pieces[0:3], left)
+        below = split(left[W:])
         for k in range(SUBS):
             at = slice(k * W, (k + 1) * W)
             half = slice(k % 2 * W, (k % 2 + 1) * W)
-            (ra, rb)[k // 2][:, half] = matrix[W:HALF, at] - dot3(below, split(right[:, at]))
-
-
-def second_panel(pieces, matrix, inverses):
-    return pl.pallas_call(
-        second_kernel,
-        in_specs=[VMEM] * 14,
-        out_specs=[VMEM] * 4,
-        out_shape=HALVES,
-        scratch_shapes=[space(FULL, W), space(W, FULL)],
-        name="second_panel",
-        **params(18 * FULL * W * W, 32 * FULL * W),
-    )(*pieces, matrix, inverses)
+            pivot = split(pieces[3 + 3 * (k // 2)][:, half])
+            (ra, rb)[k // 2][:, half] = matrix[W:HALF, at] - dot3(below, pivot)
+
+
+def second_rows(pieces, matrix, after):
+    return pl.pallas_call(
+        second_rows_kernel,
+        in_specs=[VMEM] * 10 + [ANY],
+        out_specs=[VMEM] * 2,
+        out_shape=[f32(W, HALF)] * 2,
+        scratch_shapes=[space(HALF, W)],
+        name="second_rows",
+        **params(6 * FULL * W * W, 16 * FULL * W),
+    )(*pieces[:3], *pieces[6:12], matrix, after)
 
 
 def update_rows(panel, k, matrix, out, left, high, low):
@@ -434,9 +461,12 @@
     subs = SUBS * SUBS
     strips = exchange(permute_tiles(child_tiles, destination, row_map, col_map))
     got = exchange(reduce_strips(strips, NJ * subs).reshape(NJ, subs, 2, STRIP, LANES))
-    pieces, matrix = broadcast(first_panel(parent, got, inverses), assemble(parent, got))
-    second = second_panel(pieces, matrix, inverses)
-    later, matrix = broadcast(second, update(matrix, pieces))
+    la, lb = first_factor(parent, got, inverses)
+    ra, rb = first_rows(parent, got, la)
+    pieces, matrix = broadcast((la, lb, ra, rb), assemble(parent, got))
+    la, lb = second_factor(pieces, matrix, inverses)
+    ra, rb = second_rows(pieces, matrix, la)
+    later, matrix = broadcast((la, lb, ra, rb), update(matrix, pieces))
     return finish(matrix, later)[None]
 
 

time: 236 us -> 235 us (level)
  waiting for transfers between devices: 38 us -> 34.8 us
  starting transfers between devices: 15.4 us -> 18.6 us
    ppermute x2, waiting for transfers between devices: 14.7 us -> 0.86 us  [broadcast(): lb2 = lax.ppermute(pick('col', 3, lb, lb1), 'col', PAIRS)]
    ppermute x2, waiting for transfers between devices: 13.5 us -> 0.01 us  [broadcast(): la1 = lax.ppermute(la, 'col', PAIRS)]
    ppermute x2, waiting for transfers between devices: 0.01 us -> 11.2 us  [broadcast(): ra1 = lax.ppermute(ra, 'row', PAIRS)]
    ppermute x2, waiting for transfers between devices: 2.54 us -> 9.07 us  [broadcast(): ra2 = lax.ppermute(pick('row', 1, ra, ra1), 'row', CROSS)]
    ppermute x2, waiting for transfers between devices: 0.82 us -> 5.75 us  [broadcast(): rb2 = lax.ppermute(pick('row', 3, rb, rb1), 'row', PAIRS)]
    ppermute x2, waiting for transfers between devices: 0.01 us -> 3.05 us  [broadcast(): rb1 = lax.ppermute(rb, 'row', CROSS)]
    ppermute x2, waiting for transfers between devices: 3.8 us -> 1.01 us  [broadcast(): lb1 = lax.ppermute(lb, 'col', CROSS)]
  transfers between devices with their start and end apart: 16 -> 16, of which waited for: 11 -> 12; matrix products, arithmetic and copies ran while one was open for 0% -> 0% of each run, Pallas kernels for 1% -> 2%
where the time goes in v5:
time: 235 us
  blocking collectives  161 us (69%)
  waiting for transfers between devices  34.8 us (15%)
  Pallas kernels  20.1 us (9%)
  starting transfers between devices  18.6 us (8%)
    all_to_all x2, blocking collectives, exchange(): return lax.all_to_all(value, PLANE, split_axis=0, concat_axis=0, tiled=True)  161 us
    ppermute x2, waiting for transfers between devices, broadcast(): ra1 = lax.ppermute(ra, 'row', PAIRS)  11.2 us
    ppermute x2, waiting for transfers between devices, broadcast(): ra2 = lax.ppermute(pick('row', 1, ra, ra1), 'row', CROSS)  9.07 us
    pallas_call x1, Pallas kernels, permute_tiles(): pl.pallas_call(permute_kernel, in_specs=[HBM] * 4, out_specs=HBM, out_sha...  8.31 us
    ppermute x2, waiting for transfers between devices, broadcast(): rb2 = lax.ppermute(pick('row', 3, rb, rb1), 'row', PAIRS)  5.75 us
  transfers between devices with their start and end apart: 16, of which 12 were waited for; matrix products, arithmetic and copies ran while one was open for 0% of the time, Pallas kernels for 2%

profile of v5, /device:TPU:0, one launch (start us, length us, event | category | flops | bytes accessed | tf_op | source)
XLA Modules:
  0.0 235.1 jit_solution(4926267639690750305)
XLA Ops:
  0.0 8.3 %permute.1 = f32[32,65,8,128]{3,2,1,0:T(8,128)} custom-call(s32[1,32]{1,0:T(1,128)} %bitcast.11, s32[32,256]{1,0:T(8,128)} %rows_hbm.1, s32[32,256]{1,0:T(8,128)} %cols_hbm.1, f32[32,256,256]{2,1,0:T(8,128)} %tiles_hbm.1), custom_call_target="tpu_custom_call" | custom-call | flops 4294967296 | bytes 16777216 | tf_op jit(solution)/shard_map/permute/pallas_call | solution.py:138
  8.3 106.7 %all_to_all.10.strips = f32[32,65,8,128]{3,2,1,0:T(8,128)S(1)} all-to-all(f32[32,65,8,128]{3,2,1,0:T(8,128)} %permute.1), channel_id=1, replica_groups=mesh['front'=8,'row'=4,'col'=4] {'front','row'}, dimensions={0} | all-to-all | bytes 17039360 | tf_op jit(solution)/shard_map/all_to_all | solution.py:413
  115.0 3.6 %reduce.1 = f32[512,2,8,128]{3,2,1,0:T(8,128)S(1)} custom-call(f32[32,65,8,128]{3,2,1,0:T(8,128)S(1)} %all_to_all.10.strips), custom_call_target="tpu_custom_call" | custom-call | flops 2097152 | bytes 12582912 | tf_op jit(solution)/shard_map/reduce/pallas_call | solution.py:176
  118.6 0.0 copy-start
  118.6 0.0 copy-start.1
  118.6 54.7 %all_to_all.11.got = f32[32,16,2,8,128]{4,3,2,1,0:T(8,128)S(1)} all-to-all(f32[32,16,2,8,128]{4,3,2,1,0:T(8,128)S(1)} %bitcast.8), channel_id=1, replica_groups=mesh['front'=8,'row'=4,'col'=4] {'front','row'}, dimensions={0} | all-to-all | bytes 8388608 | tf_op jit(solution)/shard_map/all_to_all | solution.py:413
  173.3 0.0 copy-done
  173.3 0.6 first_factor.1
  173.8 0.1 first_rows.1
  174.0 0.3 collective-permute-start.4
  174.3 2.1 collective-permute-start.5
  176.4 1.6 collective-permute-start
  177.9 2.2 collective-permute-start.1
  180.1 0.5 assemble.1.refs_9_.refs_12_
  180.7 6.6 %collective-permute-done.4.refs_1_.refs_7_.refs_4_ = f32[256,512]{1,0:T(8,128)S(1)} collective-permute-done((f32[256,512]{1,0:T(8,128)S(1)}, f32[256,512]{1,0:T(8,128)S(1)}, u32[]{:S(2)}, u32[]{:S(2)}) %collective-permute-start.4) | collective-permute-done | bytes 524320 | tf_op jit(solution)/shard_map/ppermute | solution.py:447
  187.3 1.5 collective-permute-done.5.refs_1_.refs_7_.refs_10_
  188.8 1.8 collective-permute-start.6
  190.6 0.0 collective-permute-done.refs_1_
  190.6 1.0 collective-permute-done.1.refs_1_.refs_4_
  191.6 2.1 collective-permute-start.2
  193.8 0.1 collective-permute-start.3
  193.9 0.1 pick.13
  194.0 0.9 collective-permute-start.11
  194.9 7.6 %collective-permute-done.6.refs_8_.refs_5_ = f32[256,512]{1,0:T(8,128)S(1)} collective-permute-done((f32[256,512]{1,0:T(8,128)S(1)}, f32[256,512]{1,0:T(8,128)S(1)}, u32[]{:S(2)}, u32[]{:S(2)}) %collective-permute-start.6) | collective-permute-done | bytes 524320 | tf_op jit(solution)/shard_map/ppermute | solution.py:452
  202.5 2.0 collective-permute-done.2.refs_2_
  204.5 0.8 collective-permute-done.3.refs_5_
  205.2 1.2 second_factor.1
  206.5 0.0 collective-permute-done.11.refs_8_.refs_11_
  206.5 0.8 second_rows.1
  207.3 0.5 collective-permute-start.12
  207.8 1.2 collective-permute-start.13
  209.0 0.9 collective-permute-start.7
  209.9 1.5 collective-permute-start.8
  211.4 2.1 update.1.refs_12_
  213.5 4.6 %collective-permute-done.12.refs_1_.refs_7_ = f32[256,512]{1,0:T(8,128)S(1)} collective-permute-done((f32[256,512]{1,0:T(8,128)S(1)}, f32[256,512]{1,0:T(8,128)S(1)}, u32[]{:S(2)}, u32[]{:S(2)}) %collective-permute-start.12) | collective-permute-done | bytes 524320 | tf_op jit(solution)/shard_map/ppermute | solution.py:447
  218.0 1.6 collective-permute-done.13.refs_1_.refs_10_
  219.7 0.1 collective-permute-start.15
  219.8 0.1 pick.14
  219.8 1.5 collective-permute-start.14
  221.3 0.0 collective-permute-done.7.refs_1_
  221.3 0.0 collective-permute-done.8.refs_1_.refs_4_
  221.4 0.6 collective-permute-start.10
  222.0 1.4 collective-permute-start.9
  223.3 5.7 %collective-permute-done.15.refs_11_ = f32[256,512]{1,0:T(8,128)S(1)} collective-permute-done((f32[256,512]{1,0:T(8,128)S(1)}, f32[256,512]{1,0:T(8,128)S(1)}, u32[]{:S(2)}, u32[]{:S(2)}) %collective-permute-start.15) | collective-permute-done | bytes 524320 | tf_op jit(solution)/shard_map/ppermute | solution.py:454
  229.1 1.5 collective-permute-done.14.refs_8_
  230.5 0.1 collective-permute-done.10.refs_5_
  230.6 1.8 collective-permute-done.9.refs_2_
  232.4 2.5 %finish.1 = f32[1024,1024]{1,0:T(8,128)} custom-call(f32[512,256]{1,0:T(8,128)S(1)} %get-tuple-element.31.refs_0_.refs_10_, f32[512,256]{1,0:T(8,128)S(1)} %collective-permute-done.7.refs_1_, f32[512,256]{1,0:T(8,128)S(1)} %collective-permute-done.9.refs_2_, f32[512,256]{1,0:T(8,128)S(1)} %get-tuple-element.32.refs_0_.refs_3_, ...), custom_call_target="tpu_custom_call" | custom-call | flops 1610612736 | bytes 10485760 | tf_op jit(solution)/shard_map/finish/pallas_call | solution.py:401
  (7 shorter events, 0.2 us)
Async XLA Ops:
  118.6 54.7 %copy-start = (f32[1,1024,1024]{2,1,0:T(8,128)S(1)}, f32[1,1024,1024]{2,1,0:T(8,128)}, u32[]{:S(2)}) copy-start(f32[1,1024,1024]{2,1,0:T(8,128)} %param.6) | copy-start | bytes 12582916
  118.6 54.7 %copy-start.1 = (f32[1,2,256,256]{3,2,1,0:T(8,128)S(1)}, f32[1,2,256,256]{3,2,1,0:T(8,128)}, u32[]{:S(2)}) copy-start(f32[1,2,256,256]{3,2,1,0:T(8,128)} %param.11) | copy-start | bytes 1572868
  174.0 13.3 %collective-permute-start.4 = (f32[256,512]{1,0:T(8,128)S(1)}, f32[256,512]{1,0:T(8,128)S(1)}, u32[]{:S(2)}, u32[]{:S(2)}) collective-permute-start(f32[256,512]{1,0:T(8,128)S(1)} %get-tuple-element.27.refs_0_.refs_6_.refs_3_), channel_id=1, source_target_pairs={{0,4},{4,0},{8,12},{12,8},{1,5},{5,1},{9,13},{13,9},{2,6},{6,2},{1... | collective-permute-start | bytes 1572872 | tf_op jit(solution)/shard_map/ppermute | solution.py:447
  174.3 14.5 %collective-permute-start.5 = (f32[256,512]{1,0:T(8,128)S(1)}, f32[256,512]{1,0:T(8,128)S(1)}, u32[]{:S(2)}, u32[]{:S(2)}) collective-permute-start(f32[256,512]{1,0:T(8,128)S(1)} %get-tuple-element.28.refs_0_.refs_6_.refs_9_), channel_id=1, source_target_pairs={{0,12},{12,0},{4,8},{8,4},{1,13},{13,1},{5,9},{9,5},{2,14},{14,2},... | collective-permute-start | bytes 1572872 | tf_op jit(solution)/shard_map/ppermute | solution.py:448
  176.4 14.2 %collective-permute-start = (f32[512,256]{1,0:T(8,128)S(1)}, f32[512,256]{1,0:T(8,128)S(1)}, u32[]{:S(2)}, u32[]{:S(2)}) collective-permute-start(f32[512,256]{1,0:T(8,128)S(1)} %get-tuple-element.23.refs_0_.after), channel_id=1, source_target_pairs={{0,1},{1,0},{2,3},{3,2},{4,5},{5,4},{6,7},{7,6},{8,9},{9,8},{10,11... | collective-permute-start | bytes 1572872 | tf_op jit(solution)/shard_map/ppermute | solution.py:445
  177.9 13.7 %collective-permute-start.1 = (f32[512,256]{1,0:T(8,128)S(1)}, f32[512,256]{1,0:T(8,128)S(1)}, u32[]{:S(2)}, u32[]{:S(2)}) collective-permute-start(f32[512,256]{1,0:T(8,128)S(1)} %get-tuple-element.24.refs_0_.refs_3_), channel_id=1, source_target_pairs={{0,3},{3,0},{1,2},{2,1},{4,7},{7,4},{5,6},{6,5},{8,11},{11,8},{9,1... | collective-permute-start | bytes 1572872 | tf_op jit(solution)/shard_map/ppermute | solution.py:446
  188.8 13.7 %collective-permute-start.6 = (f32[256,512]{1,0:T(8,128)S(1)}, f32[256,512]{1,0:T(8,128)S(1)}, u32[]{:S(2)}, u32[]{:S(2)}) collective-permute-start(f32[256,512]{1,0:T(8,128)S(1)} %pick.10), channel_id=1, source_target_pairs={{0,12},{12,0},{4,8},{8,4},{1,13},{13,1},{5,9},{9,5},{2,14},{14,2},... | collective-permute-start | bytes 1572872 | tf_op jit(solution)/shard_map/ppermute | solution.py:452
  191.6 12.8 %collective-permute-start.2 = (f32[512,256]{1,0:T(8,128)S(1)}, f32[512,256]{1,0:T(8,128)S(1)}, u32[]{:S(2)}, u32[]{:S(2)}) collective-permute-start(f32[512,256]{1,0:T(8,128)S(1)} %pick.8), channel_id=1, source_target_pairs={{0,3},{3,0},{1,2},{2,1},{4,7},{7,4},{5,6},{6,5},{8,11},{11,8},{9,1... | collective-permute-start | bytes 1572872 | tf_op jit(solution)/shard_map/ppermute | solution.py:451
  193.8 11.4 %collective-permute-start.3 = (f32[512,256]{1,0:T(8,128)S(1)}, f32[512,256]{1,0:T(8,128)S(1)}, u32[]{:S(2)}, u32[]{:S(2)}) collective-permute-start(f32[512,256]{1,0:T(8,128)S(1)} %pick.9), channel_id=1, source_target_pairs={{0,1},{1,0},{2,3},{3,2},{4,5},{5,4},{6,7},{7,6},{8,9},{9,8},{10,11... | collective-permute-start | bytes 1572872 | tf_op jit(solution)/shard_map/ppermute | solution.py:453
  194.0 12.5 %collective-permute-start.11 = (f32[256,512]{1,0:T(8,128)S(1)}, f32[256,512]{1,0:T(8,128)S(1)}, u32[]{:S(2)}, u32[]{:S(2)}) collective-permute-start(f32[256,512]{1,0:T(8,128)S(1)} %pick.13), channel_id=1, source_target_pairs={{0,4},{4,0},{8,12},{12,8},{1,5},{5,1},{9,13},{13,9},{2,6},{6,2},{1... | collective-permute-start | bytes 1572872 | tf_op jit(solution)/shard_map/ppermute | solution.py:454
  207.3 10.7 %collective-permute-start.12 = (f32[256,512]{1,0:T(8,128)S(1)}, f32[256,512]{1,0:T(8,128)S(1)}, u32[]{:S(2)}, u32[]{:S(2)}) collective-permute-start(f32[256,512]{1,0:T(8,128)S(1)} %get-tuple-element.36.refs_0_.refs_6_), channel_id=1, source_target_pairs={{0,4},{4,0},{8,12},{12,8},{1,5},{5,1},{9,13},{13,9},{2,6},{6,2},{1... | collective-permute-start | bytes 1572872 | tf_op jit(solution)/shard_map/ppermute | solution.py:447
  207.8 11.8 %collective-permute-start.13 = (f32[256,512]{1,0:T(8,128)S(1)}, f32[256,512]{1,0:T(8,128)S(1)}, u32[]{:S(2)}, u32[]{:S(2)}) collective-permute-start(f32[256,512]{1,0:T(8,128)S(1)} %get-tuple-element.37.refs_0_.refs_9_), channel_id=1, source_target_pairs={{0,12},{12,0},{4,8},{8,4},{1,13},{13,1},{5,9},{9,5},{2,14},{14,2},... | collective-permute-start | bytes 1572872 | tf_op jit(solution)/shard_map/ppermute | solution.py:448
  209.0 12.3 %collective-permute-start.7 = (f32[512,256]{1,0:T(8,128)S(1)}, f32[512,256]{1,0:T(8,128)S(1)}, u32[]{:S(2)}, u32[]{:S(2)}) collective-permute-start(f32[512,256]{1,0:T(8,128)S(1)} %get-tuple-element.31.refs_0_.refs_10_), channel_id=1, source_target_pairs={{0,1},{1,0},{2,3},{3,2},{4,5},{5,4},{6,7},{7,6},{8,9},{9,8},{10,11... | collective-permute-start | bytes 1572872 | tf_op jit(solution)/shard_map/ppermute | solution.py:445
  209.9 11.4 %collective-permute-start.8 = (f32[512,256]{1,0:T(8,128)S(1)}, f32[512,256]{1,0:T(8,128)S(1)}, u32[]{:S(2)}, u32[]{:S(2)}) collective-permute-start(f32[512,256]{1,0:T(8,128)S(1)} %get-tuple-element.32.refs_0_.refs_3_), channel_id=1, source_target_pairs={{0,3},{3,0},{1,2},{2,1},{4,7},{7,4},{5,6},{6,5},{8,11},{11,8},{9,1... | collective-permute-start | bytes 1572872 | tf_op jit(solution)/shard_map/ppermute | solution.py:446
  219.7 9.4 %collective-permute-start.15 = (f32[256,512]{1,0:T(8,128)S(1)}, f32[256,512]{1,0:T(8,128)S(1)}, u32[]{:S(2)}, u32[]{:S(2)}) collective-permute-start(f32[256,512]{1,0:T(8,128)S(1)} %pick.15), channel_id=1, source_target_pairs={{0,4},{4,0},{8,12},{12,8},{1,5},{5,1},{9,13},{13,9},{2,6},{6,2},{1... | collective-permute-start | bytes 1572872 | tf_op jit(solution)/shard_map/ppermute | solution.py:454
  219.8 10.7 %collective-permute-start.14 = (f32[256,512]{1,0:T(8,128)S(1)}, f32[256,512]{1,0:T(8,128)S(1)}, u32[]{:S(2)}, u32[]{:S(2)}) collective-permute-start(f32[256,512]{1,0:T(8,128)S(1)} %pick.14), channel_id=1, source_target_pairs={{0,12},{12,0},{4,8},{8,4},{1,13},{13,1},{5,9},{9,5},{2,14},{14,2},... | collective-permute-start | bytes 1572872 | tf_op jit(solution)/shard_map/ppermute | solution.py:452
  221.4 9.3 %collective-permute-start.10 = (f32[512,256]{1,0:T(8,128)S(1)}, f32[512,256]{1,0:T(8,128)S(1)}, u32[]{:S(2)}, u32[]{:S(2)}) collective-permute-start(f32[512,256]{1,0:T(8,128)S(1)} %pick.12), channel_id=1, source_target_pairs={{0,1},{1,0},{2,3},{3,2},{4,5},{5,4},{6,7},{7,6},{8,9},{9,8},{10,11... | collective-permute-start | bytes 1572872 | tf_op jit(solution)/shard_map/ppermute | solution.py:453
  222.0 10.5 %collective-permute-start.9 = (f32[512,256]{1,0:T(8,128)S(1)}, f32[512,256]{1,0:T(8,128)S(1)}, u32[]{:S(2)}, u32[]{:S(2)}) collective-permute-start(f32[512,256]{1,0:T(8,128)S(1)} %pick.11), channel_id=1, source_target_pairs={{0,3},{3,0},{1,2},{2,1},{4,7},{7,4},{5,6},{6,5},{8,11},{11,8},{9,1... | collective-permute-start | bytes 1572872 | tf_op jit(solution)/shard_map/ppermute | solution.py:451
